TPU v7x, 32 devices: a whole 2x2x4 slice. The times are simulated.
32 devices in a mesh: polar: 4 (over x, core), azimuth: 8 (over z, y).
Axes of the slice: x: 2, y: 2, z: 4, core: 2. Of those that a mesh axis runs over, the one named last changes fastest.
Arguments:
- field: float32 [1, 128, 192, 384], P(None, 'polar', 'azimuth'), may hold values from -6 to 6
- filter_real: float32 [64, 384, 384], P('azimuth'), may hold values from -0.3125 to 0.3125
- filter_imag: float32 [64, 384, 384], P('azimuth'), may hold values from -0.3125 to 0.3125
- norm_gain: float32 [384], replicated, may hold values from 0.1 to 1.9
- w_in: bfloat16 [384, 768], replicated, may hold values from -0.3125 to 0.3125
- w_out: bfloat16 [768, 384], replicated, may hold values from -0.21875 to 0.21875
Outputs:
- mixed: float32 [1, 64, 96, 384], P(None, 'polar', 'azimuth')
All inputs are finite; a program needn't handle non-finite values.
Results may differ from a plain program's by a relative error of at most 0.0035.
Values sent between devices are 32-bit elements; how exact they have to be, the bound alone decides.
No kernel may reach another device: no remote copies, remote signals or barrier semaphores. Data moves between devices by JAX's collectives and lax.ppermute only.
A program may use at most 128 MiB of HBM per device.

v0:
```python
import functools
import math

import jax
import jax.numpy as jnp
import numpy as np
from jax import lax
from jax.experimental import pallas as pl
from jax.experimental.pallas import tpu as pltpu
from jax.sharding import PartitionSpec as P


def legendre(nodes, degrees, orders):
    cosines, sines = np.cos(nodes)[None, :], np.sin(nodes)[None, :]
    mode = np.arange(orders, dtype=np.float64)[:, None]
    counter = np.arange(1, orders + 1, dtype=np.float64)
    ratios = np.log((2.0 * counter - 1.0) / (2.0 * counter))
    product_log = np.concatenate([[0.0], np.cumsum(ratios)])[:orders, None]
    diagonal = np.exp(
        0.5 * (np.log((2.0 * mode + 1.0) / (4.0 * math.pi)) + product_log) + mode * np.log(sines)
    )
    newest, older = np.zeros_like(diagonal), np.zeros_like(diagonal)
    stacked = []
    for degree in range(degrees):
        lower = np.where(degree > mode, degree * degree - mode * mode, 1.0)
        factor_a = np.sqrt(max(4.0 * degree * degree - 1.0, 0.0) / lower)
        factor_b = np.sqrt(
            np.maximum((degree - 1.0) ** 2 - mode**2, 0.0) / max(4.0 * (degree - 1.0) ** 2 - 1.0, 1.0)
        )
        recurred = factor_a * (cosines * newest - factor_b * older)
        second = np.sqrt(2.0 * mode + 3.0) * cosines * newest
        value = np.where(
            degree == mode,
            diagonal,
            np.where(degree == mode + 1.0, second, np.where(degree > mode + 1.0, recurred, 0.0)),
        )
        stacked.append(value)
        newest, older = value, newest
    return np.stack(stacked, axis=1)


def colatitudes(count):
    return math.pi * (np.arange(count) + 0.5) / count


def fourier_table(points, mode_ids, halves, weights):
    angle = 2.0 * math.pi / points * (np.arange(points)[:, None] * mode_ids[None, :] % points)
    return np.where(
        halves[None, :] == 0, weights[None, :] * np.cos(angle), -weights[None, :] * np.sin(angle)
    )


def by_axes(field, filter_real, filter_imag, norm_gain, w_in, w_out):
    high = lax.Precision.HIGHEST
    samples, lat_rows, lon_cols, channels = field.shape
    polar_count = lax.axis_size("polar")
    azimuth_count = lax.axis_size("azimuth")
    fine_lat = lat_rows * polar_count
    fine_lon = lon_cols * azimuth_count
    coarse_lat = fine_lat // 2
    coarse_lon = fine_lon // 2
    orders = coarse_lon // 2
    order_piece = orders // polar_count
    chan_slice = channels // azimuth_count
    columns_all = np.arange(2 * orders)
    halves = columns_all // order_piece % 2
    mode_ids = columns_all // (2 * order_piece) * order_piece + columns_all % order_piece
    twofold = np.where(mode_ids == 0, 1.0, 2.0)
    forward_table = jnp.asarray(
        fourier_table(fine_lon, mode_ids, halves, np.ones(2 * orders)), jnp.float32
    )
    inverse_table = jnp.asarray(fourier_table(coarse_lon, mode_ids, halves, twofold).T, jnp.float32)
    polar_index = lax.axis_index("polar")
    fine_nodes = colatitudes(fine_lat)
    quadrature = math.pi / fine_lat * np.sin(fine_nodes) * (2.0 * math.pi / fine_lon)
    all_fine = legendre(fine_nodes, coarse_lat, orders) * quadrature
    all_coarse = legendre(colatitudes(coarse_lat), coarse_lat, orders)
    own_orders = lambda table: lax.dynamic_slice_in_dim(
        jnp.asarray(table, jnp.float32), polar_index * order_piece, order_piece, 0
    )
    table_fine = own_orders(all_fine)
    table_coarse = own_orders(all_coarse)
    moved = lax.all_to_all(field, "azimuth", split_axis=3, concat_axis=2, tiled=True)
    spectrum = jnp.einsum("bijc,jk->bick", moved, forward_table, precision=high)
    by_order = lax.all_to_all(spectrum, "polar", split_axis=3, concat_axis=1, tiled=True)
    by_order = by_order.reshape(samples, fine_lat, chan_slice, 2, order_piece)
    coef = jnp.einsum("kli,bicpk->blcpk", table_fine, by_order, precision=high)
    degree_block = lax.all_to_all(coef, "azimuth", split_axis=1, concat_axis=2, tiled=True)
    block_re = degree_block[:, :, :, 0]
    block_im = degree_block[:, :, :, 1]
    out_re = jnp.einsum("lco,blck->blok", filter_real, block_re, precision=high) - jnp.einsum(
        "lco,blck->blok", filter_imag, block_im, precision=high
    )
    out_im = jnp.einsum("lco,blck->blok", filter_real, block_im, precision=high) + jnp.einsum(
        "lco,blck->blok", filter_imag, block_re, precision=high
    )
    mixed_spec = jnp.stack([out_re, out_im], axis=3)
    filtered = lax.all_to_all(mixed_spec, "azimuth", split_axis=2, concat_axis=1, tiled=True)
    both_fields = jnp.concatenate([coef, filtered], axis=2)
    grid_modes = jnp.einsum("kli,blcpk->bicpk", table_coarse, both_fields, precision=high)
    grid_modes = grid_modes.reshape(samples, coarse_lat, 2 * chan_slice, 2 * order_piece)
    row_block = lax.all_to_all(grid_modes, "polar", split_axis=1, concat_axis=3, tiled=True)
    values = jnp.einsum("bick,kj->bijc", row_block, inverse_table, precision=high)
    state_split = (
        jax.nn.gelu(values[..., chan_slice:], approximate=False) + values[..., :chan_slice]
    )
    state = lax.all_to_all(state_split, "azimuth", split_axis=2, concat_axis=3, tiled=True)
    center = jnp.mean(state, axis=-1, keepdims=True)
    spread = jnp.mean((state - center) ** 2, axis=-1, keepdims=True)
    normed = ((state - center) * lax.rsqrt(spread + 1e-05) * norm_gain).astype(jnp.bfloat16)
    flat = normed.reshape(-1, channels)
    hidden = jax.nn.gelu(
        jnp.dot(flat, w_in, preferred_element_type=jnp.float32), approximate=False
    ).astype(jnp.bfloat16)
    update = jnp.dot(hidden, w_out, preferred_element_type=jnp.float32)
    return state + update.reshape(state.shape)


LANES = 128
BOTH = ("polar", "azimuth")
MIB = 1024 * 1024


def split_bf16(table):
    high = table.astype(jnp.bfloat16)
    return high, (table - high.astype(jnp.float32)).astype(jnp.bfloat16)


def split_constant(table):
    table = np.asarray(table, np.float32)
    high = table.astype(jnp.bfloat16)
    return jnp.asarray(high), jnp.asarray((table - high.astype(np.float32)).astype(jnp.bfloat16))


def dot(left, right):
    return jnp.dot(left, right, preferred_element_type=jnp.float32)


def dot3(left, right_high, right_low):
    rows = left.shape[0]
    left_high, left_low = split_bf16(left)
    both = dot(jnp.concatenate([left_high, left_low], axis=0), right_high)
    return both[:rows] + both[rows:] + dot(left_high, right_low)


def swap(blocks, bits):
    lane = lax.broadcasted_iota(jnp.int32, blocks[0].shape, len(blocks[0].shape) - 1)
    axis = len(blocks[0].shape) - 1
    blocks = list(blocks)
    for order, bit in enumerate(bits):
        step = 1 << bit
        keep = (lane & step) == 0
        for index in range(len(blocks)):
            if index >> order & 1:
                continue
            first, second = blocks[index], blocks[index | 1 << order]
            blocks[index] = jnp.where(keep, first, pltpu.roll(second, step, axis))
            blocks[index | 1 << order] = jnp.where(
                keep, pltpu.roll(first, LANES - step, axis), second
            )
    return blocks


OWNER_BITS = (0, 1, 2, 3, 6)
QUAD_BITS = (4, 5)
LOW_BITS = (0, 1, 2, 3, 4)


def gelu(values):
    return 0.5 * values * (1.0 + lax.erf(values * math.sqrt(0.5)))


def scatter_kernel(field, sent):
    devices, rows, channels = sent.shape
    for tile in range(channels // LANES):
        lanes = pl.ds(tile * LANES, LANES)
        blocks = swap([field[0, lat, :, lanes] for lat in range(devices)], OWNER_BITS)
        for device in range(devices):
            sent[device, :, lanes] = blocks[device]


def analysis_kernel(
    polar_count, got, four_high, four_low, leg_high, leg_low, coef, sent, rows, high_buf, low_buf, sems
):
    copies = [
        pltpu.make_async_copy(leg_high, high_buf, sems.at[0]),
        pltpu.make_async_copy(leg_low, low_buf, sems.at[1]),
    ]
    for copy in copies:
        copy.start()
    devices, lon_cols, width = got.shape
    azimuth_count = devices // polar_count
    modes = four_high.shape[0]
    orders = modes // 2
    four = jnp.concatenate([four_high[...], four_low[...]], axis=0)
    tiles = width // LANES
    for tile in range(tiles):
        spectra = []
        for polar in range(polar_count):
            block = got[pl.ds(polar * azimuth_count, azimuth_count), :, pl.ds(tile * LANES, LANES)]
            block = block.reshape(azimuth_count * lon_cols, LANES)
            block_high, block_low = split_bf16(block)
            both = dot(four, block_high)
            spectra.append(both[:modes] + both[modes:] + dot(four[:modes], block_low))
        for quad, spectrum in enumerate(swap(spectra, QUAD_BITS)):
            rows[pl.ds((tile * polar_count + quad) * modes, modes), :] = spectrum
    for copy in copies:
        copy.wait()
    pairs = orders // 2
    count = 2 * tiles * polar_count
    for pair in range(pairs):
        first = rows[pl.ds(pair, count, stride=orders), :]
        second = rows[pl.ds(pairs + pair, count, stride=orders), :]
        coef[pair] = dot3(jnp.concatenate([first, second], axis=1), high_buf[pair], low_buf[pair])
    pack_by_degree(coef, sent)


def pack_by_degree(coef, sent):
    devices, count, _ = sent.shape
    pairs = coef.shape[0]
    for row in range(0, count, 8):
        part = pl.ds(row, 8)
        zero = jnp.zeros((8, LANES), jnp.float32)
        blocks = swap(
            [coef[pair, part, :] if pair < pairs else zero for pair in range(devices)], LOW_BITS
        )
        for device in range(devices):
            sent[device, part, :] = blocks[device]


def filter_kernel(first_degree, got, real, imag, sent, real_buf, imag_buf, turned, sems):
    degrees, channels, _ = real_buf.shape
    start = first_degree[0]
    copies = []
    for degree in range(degrees):
        pair = [
            pltpu.make_async_copy(real.at[start + degree], real_buf.at[degree], sems.at[0, degree]),
            pltpu.make_async_copy(imag.at[start + degree], imag_buf.at[degree], sems.at[1, degree]),
        ]
        for copy in pair:
            copy.start()
        copies.append(pair)
    devices, count, _ = sent.shape
    tiles = channels // LANES
    groups = [
        (tile, top, quad) for tile in range(tiles) for top in range(2) for quad in range(4)
    ]
    spectra = []
    for half in range(2):
        parts = [
            got[pl.ds(top * 16 * count + 2 * (4 * tile + quad) + half, 16, stride=count), :]
            for tile, top, quad in groups
        ]
        spectra.append(jnp.concatenate(parts, axis=0).T)
    pad = LANES // (2 * degrees)
    results = [[None] * (2 * degrees) for _ in range(2)]
    for degree in range(degrees):
        for copy in copies[degree]:
            copy.wait()
        own = jnp.concatenate(
            [
                spectra[half][(order * degrees + degree) * pad : (order * degrees + degree + 1) * pad]
                for half in range(2)
                for order in range(2)
            ],
            axis=0,
        )
        by_real = dot3(own, *split_bf16(real_buf[degree]))
        by_imag = dot3(own, *split_bf16(imag_buf[degree]))
        size = 2 * pad
        out_re = by_real[:size] - by_imag[size:]
        out_im = by_real[size:] + by_imag[:size]
        for order in range(2):
            results[0][order * degrees + degree] = out_re[order * pad : (order + 1) * pad]
            results[1][order * degrees + degree] = out_im[order * pad : (order + 1) * pad]
    for half in range(2):
        across = jnp.concatenate(results[half], axis=0).T
        for place, (tile, top, quad) in enumerate(groups):
            turned[pl.ds(((top * tiles * 4 + 4 * tile + quad) * 2 + half) * 16, 16), :] = across[
                place * 16 : (place + 1) * 16
            ]
    for device in range(devices):
        sent[device] = turned[pl.ds(device // 16 * 16 * count + device % 16, count, stride=16), :]


def synthesis_kernel(
    polar_count, got, coef, four_high, four_low, leg_high, leg_low, sent, back, modes_buf,
    high_buf, low_buf, sems
):
    copies = [
        pltpu.make_async_copy(leg_high, high_buf, sems.at[0]),
        pltpu.make_async_copy(leg_low, low_buf, sems.at[1]),
    ]
    for copy in copies:
        copy.start()
    devices, count, _ = got.shape
    azimuth_count = devices // polar_count
    pairs = coef.shape[0]
    orders = 2 * pairs
    for row in range(0, count, 8):
        part = pl.ds(row, 8)
        blocks = swap([got[device, part, :] for device in range(devices)], LOW_BITS)
        for pair in range(pairs):
            back[pair, part, :] = blocks[pair]
    for copy in copies:
        copy.wait()
    keep = (lax.broadcasted_iota(jnp.int32, (count, LANES), 1) & 64) == 0
    for pair in range(pairs):
        both = jnp.concatenate([coef[pair], back[pair]], axis=0)
        values = dot3(both, high_buf[pair], low_buf[pair])
        for order in range(2):
            lanes = slice(order * LANES, (order + 1) * LANES)
            modes_buf[pl.ds((order * pairs + pair) * count, count), :] = jnp.where(
                keep, values[:count, lanes], values[count:, lanes]
            )
    four = jnp.concatenate([four_high[...], four_low[...]], axis=0)
    points = four_high.shape[0]
    half = points // 2
    keep = (lax.broadcasted_iota(jnp.int32, (half, LANES), 1) & 64) == 0
    for tile in range(count // 8):
        states = []
        for quad in range(4):
            row = 2 * (4 * tile + quad)
            modes = jnp.concatenate(
                [modes_buf[pl.ds(row + part, orders, stride=count), :] for part in range(2)], axis=0
            )
            modes_high, modes_low = split_bf16(modes)
            both = dot(four, modes_high)
            values = both[:points] + both[points:] + dot(four[:points], modes_low)
            first, second = values[:half], values[half:]
            skip = jnp.where(keep, first, pltpu.roll(second, 64, 1))
            branch = jnp.where(keep, pltpu.roll(first, 64, 1), second)
            states.append(gelu(branch) + skip)
        for polar, state in enumerate(swap(states, QUAD_BITS)):
            for azimuth in range(azimuth_count):
                sent[polar * azimuth_count + azimuth, pl.ds(8 * tile, 8), :] = state[
                    8 * azimuth : 8 * azimuth + 8
                ]


def mlp_kernel(got, gain, w_in, w_out, mixed, state):
    devices, count, _ = got.shape
    tiles = count // 8
    for tile in range(tiles):
        blocks = swap([got[device, pl.ds(8 * tile, 8), :] for device in range(devices)], OWNER_BITS)
        for device in range(devices):
            state[pl.ds(8 * device, 8), pl.ds(tile * LANES, LANES)] = blocks[device]
    value = state[...]
    center = jnp.mean(value, axis=-1, keepdims=True)
    spread = jnp.mean((value - center) ** 2, axis=-1, keepdims=True)
    normed = ((value - center) * lax.rsqrt(spread + 1e-05) * gain[...]).astype(jnp.bfloat16)
    hidden = gelu(dot(normed, w_in[...])).astype(jnp.bfloat16)
    state[...] = value + dot(hidden, w_out[...])
    _, lat_rows, lon_cols, _ = mixed.shape
    part = lon_cols // 2
    for top in range(2):
        for lat in range(lat_rows):
            row = 8 * (top * lat_rows + lat)
            mixed[0, lat, pl.ds(top * part, part), :] = state[pl.ds(row, part), :]


def joint_fits(field, filter_real, polar_count, azimuth_count):
    samples, lat_rows, lon_cols, channels = field.shape
    devices = polar_count * azimuth_count
    orders = lon_cols * azimuth_count // 4
    return (
        samples == 1
        and devices == 32
        and polar_count == 4
        and lat_rows == 32
        and lon_cols % 8 == 0
        and lon_cols // 4 <= 8
        and channels % LANES == 0
        and filter_real.shape[0] == 2 * polar_count
        and orders % 16 == 0
        and orders // 2 <= 32
    )


def jointly(field, filter_real, filter_imag, norm_gain, w_in, w_out):
    _, lat_rows, lon_cols, channels = field.shape
    polar_count = lax.axis_size("polar")
    azimuth_count = lax.axis_size("azimuth")
    devices = polar_count * azimuth_count
    fine_lat, fine_lon = lat_rows * polar_count, lon_cols * azimuth_count
    coarse_lat, coarse_lon = fine_lat // 2, fine_lon // 2
    orders = coarse_lon // 2
    pairs = orders // 2
    tiles = channels // LANES
    count = 2 * channels // devices
    degrees_here = coarse_lat // devices
    lat_out, lon_out = coarse_lat // polar_count, coarse_lon // azimuth_count

    mode_ids = np.tile(np.arange(orders), 2)
    halves = np.repeat(np.arange(2), orders)
    forward = fourier_table(fine_lon, mode_ids, halves, np.ones(2 * orders)).T
    twofold = np.where(mode_ids == 0, 1.0, 2.0)
    inverse = fourier_table(coarse_lon, mode_ids, halves, twofold)
    backward = np.zeros((2, azimuth_count, 8, 2 * orders))
    backward[:, :, : lon_out // 2] = inverse.reshape(
        azimuth_count, 2, lon_out // 2, 2 * orders
    ).transpose(1, 0, 2, 3)
    backward = backward.reshape(-1, 2 * orders)

    fine_nodes = colatitudes(fine_lat)
    quadrature = math.pi / fine_lat * np.sin(fine_nodes) * (2.0 * math.pi / fine_lon)
    fine = legendre(fine_nodes, coarse_lat, orders) * quadrature
    coarse = legendre(colatitudes(coarse_lat), coarse_lat, orders)
    owner = np.arange(devices)
    degree = (
        owner % azimuth_count * (coarse_lat // azimuth_count) + owner // azimuth_count * degrees_here
    )
    degree = (degree[None, :] + np.arange(degrees_here)[:, None]).reshape(-1)
    lane = np.arange(LANES)
    lat_fine = (lane >> 4 & 3) * lat_rows + (lane >> 6) * 16 + (lane & 15)
    lat_coarse = (lane >> 4 & 3) * lat_out + (lane & 15)
    fine = fine[:, degree][:, :, lat_fine].transpose(0, 2, 1)
    coarse = coarse[:, degree][:, :, lat_coarse]
    size = degree.shape[0]
    analyse = np.zeros((pairs, 2, LANES, 2, size))
    synthesise = np.zeros((pairs, 2, size, 2, LANES))
    for order in range(2):
        analyse[:, order, :, order, :] = fine[order * pairs : (order + 1) * pairs]
        synthesise[:, order, :, order, :] = coarse[order * pairs : (order + 1) * pairs]
    analyse = analyse.reshape(pairs, 2 * LANES, 2 * size)
    synthesise = synthesise.reshape(pairs, 2 * size, 2 * LANES)

    vmem = pl.BlockSpec(memory_space=pltpu.VMEM)
    anywhere = pl.BlockSpec(memory_space=pl.ANY)
    block = jax.ShapeDtypeStruct((devices, count, LANES), jnp.float32)
    exchange = functools.partial(
        lax.all_to_all, axis_name=BOTH, split_axis=0, concat_axis=0, tiled=True
    )

    sent = pl.pallas_call(
        scatter_kernel,
        grid=(lon_cols // 8,),
        in_specs=[pl.BlockSpec((1, lat_rows, 8, channels), lambda step: (0, 0, step, 0))],
        out_specs=pl.BlockSpec((devices, 8, channels), lambda step: (0, step, 0)),
        out_shape=jax.ShapeDtypeStruct((devices, lon_cols, channels), jnp.float32),
        compiler_params=pltpu.CompilerParams(vmem_limit_bytes=8 * MIB),
        name="scatter_channels",
    )(field)
    got = exchange(sent)
    table_buf = pltpu.VMEM(analyse.shape, jnp.bfloat16)
    coef, sent = pl.pallas_call(
        functools.partial(analysis_kernel, polar_count),
        in_specs=[vmem, vmem, vmem, anywhere, anywhere],
        out_specs=[vmem, vmem],
        out_shape=[jax.ShapeDtypeStruct((pairs, count, LANES), jnp.float32), block],
        scratch_shapes=[
            pltpu.VMEM((count * orders, LANES), jnp.float32),
            table_buf,
            table_buf,
            pltpu.SemaphoreType.DMA((2,)),
        ],
        compiler_params=pltpu.CompilerParams(vmem_limit_bytes=16 * MIB),
        name="analysis",
    )(got, *split_constant(forward), *split_constant(analyse))
    got = exchange(sent)
    first_degree = (lax.axis_index("polar") * degrees_here).astype(jnp.int32).reshape(1)
    sent = pl.pallas_call(
        filter_kernel,
        in_specs=[pl.BlockSpec(memory_space=pltpu.SMEM), vmem, anywhere, anywhere],
        out_specs=vmem,
        out_shape=block,
        scratch_shapes=[
            pltpu.VMEM((degrees_here, channels, channels), jnp.float32),
            pltpu.VMEM((degrees_here, channels, channels), jnp.float32),
            pltpu.VMEM((2 * channels, LANES), jnp.float32),
            pltpu.SemaphoreType.DMA((2, degrees_here)),
        ],
        compiler_params=pltpu.CompilerParams(vmem_limit_bytes=16 * MIB),
        name="channel_filter",
    )(first_degree, got.reshape(devices * count, LANES), filter_real, filter_imag)
    got = exchange(sent)
    table_buf = pltpu.VMEM(synthesise.shape, jnp.bfloat16)
    sent = pl.pallas_call(
        functools.partial(synthesis_kernel, polar_count),
        in_specs=[vmem, vmem, vmem, vmem, anywhere, anywhere],
        out_specs=vmem,
        out_shape=block,
        scratch_shapes=[
            pltpu.VMEM((pairs, count, LANES), jnp.float32),
            pltpu.VMEM((orders * count, LANES), jnp.float32),
            table_buf,
            table_buf,
            pltpu.SemaphoreType.DMA((2,)),
        ],
        compiler_params=pltpu.CompilerParams(vmem_limit_bytes=16 * MIB),
        name="synthesis",
    )(got, coef, *split_constant(backward), *split_constant(synthesise))
    got = exchange(sent)
    return pl.pallas_call(
        mlp_kernel,
        in_specs=[vmem] * 4,
        out_specs=vmem,
        out_shape=jax.ShapeDtypeStruct((1, lat_out, lon_out, channels), jnp.float32),
        scratch_shapes=[pltpu.VMEM((8 * devices, channels), jnp.float32)],
        compiler_params=pltpu.CompilerParams(vmem_limit_bytes=16 * MIB),
        name="mlp",
    )(got, norm_gain.reshape(1, channels), w_in, w_out)


def per_device(field, filter_real, filter_imag, norm_gain, w_in, w_out):
    polar_count, azimuth_count = lax.axis_size("polar"), lax.axis_size("azimuth")
    plan = jointly if joint_fits(field, filter_real, polar_count, azimuth_count) else by_axes
    return plan(field, filter_real, filter_imag, norm_gain, w_in, w_out)


def solution(mesh):
    in_specs = (
        P(None, "polar", "azimuth", None),
        P("azimuth", None, None),
        P("azimuth", None, None),
        P(),
        P(),
        P(),
    )
    out_specs = P(None, "polar", "azimuth", None)
    return jax.shard_map(
        per_device, mesh=mesh, in_specs=in_specs, out_specs=out_specs, check_vma=False
    )
```

profile of v0, /device:TPU:0, one launch (start us, length us, event | category | flops | bytes accessed | tf_op | source)
XLA Modules:
  0.0 104.9 jit_solution(6930111707657743076)
XLA Ops:
  0.0 1.3 %copy-done.6 = f32[1,32,24,384]{3,2,1,0:T(8,128)S(1)} copy-done((f32[1,32,24,384]{3,2,1,0:T(8,128)S(1)}, f32[1,32,24,384]{3,2,1,0:T(8,128)}, u32[]{:S(2)}) %copy-start.6) | copy-done | bytes 1179672
  1.3 2.9 %scatter_channels.1 = f32[32,24,384]{2,1,0:T(8,128)S(1)} custom-call(f32[1,32,24,384]{3,2,1,0:T(8,128)S(1)} %copy-done.6), custom_call_target="tpu_custom_call" | custom-call | tf_op jit(solution)/shard_map/scatter_channels/pallas_call | solution.py:435
  4.2 0.0 copy-start.4
  4.2 0.0 copy-start.9
  4.2 0.0 copy-start.10
  4.2 37.5 %all_to_all.20.got = f32[32,24,384]{2,1,0:T(8,128)S(1)} all-to-all(f32[32,24,384]{2,1,0:T(8,128)S(1)} %scatter_channels.1), channel_id=1, replica_groups=mesh['polar'=4,'azimuth'=8] {'polar','azimuth'}, dimensions={0} | all-to-all | bytes 2359296 | tf_op jit(solution)/shard_map/all_to_all | solution.py:444
  41.7 0.0 copy-done.5
  41.7 0.0 copy-done.4
  41.7 0.0 copy-done.9
  41.7 0.0 copy-done.10
  41.7 2.8 %analysis.1 = (f32[24,24,128]{2,1,0:T(8,128)S(1)}, f32[32,24,128]{2,1,0:T(8,128)}) custom-call(f32[32,24,384]{2,1,0:T(8,128)S(1)} %all_to_all.20.got, bf16[96,192]{1,0:T(8,128)(2,1)S(1)} %copy-done.9, bf16[96,192]{1,0:T(8,128)(2,1)S(1)} %copy-done.10, bf16[24,256,128]{2,1,0:T(8,128)(2,1)S(1)} %copy-done.4, bf16[24,256,128]{2,1,0:T(8,128)(2,1)S(1)} %copy-done.5), custom_call_target="tpu_custom_call" | custom-call | tf_op jit(solution)/shard_map/analysis/pallas_call | solution.py:446
  44.6 2.6 %all-to-all-start.1 = ((f32[32,24,128]{2,1,0:T(8,128)}), f32[32,24,128]{2,1,0:T(8,128)S(1)}, u32[]{:S(2)}, u32[]{:S(2)}) async-start(f32[32,24,128]{2,1,0:T(8,128)} %get-tuple-element.7), calls=%async_computation.1 | async-start | bytes 786432 | tf_op jit(solution)/shard_map/all_to_all | solution.py:460
  47.2 13.5 %all-to-all-done.1 = f32[32,24,128]{2,1,0:T(8,128)S(1)} async-done(((f32[32,24,128]{2,1,0:T(8,128)}), f32[32,24,128]{2,1,0:T(8,128)S(1)}, u32[]{:S(2)}, u32[]{:S(2)}) %all-to-all-start.1) | async-done | bytes 393248 | tf_op jit(solution)/shard_map/all_to_all | solution.py:460
  60.7 2.3 %copy-done = f32[8,384,384]{2,1,0:T(8,128)S(1)} copy-done((f32[8,384,384]{2,1,0:T(8,128)S(1)}, f32[8,384,384]{2,1,0:T(8,128)}, u32[]{:S(2)}) %copy-start) | copy-done | bytes 4718616
  63.1 2.3 %copy-done.1 = f32[8,384,384]{2,1,0:T(8,128)S(1)} copy-done((f32[8,384,384]{2,1,0:T(8,128)S(1)}, f32[8,384,384]{2,1,0:T(8,128)}, u32[]{:S(2)}) %copy-start.1) | copy-done | bytes 4718616
  65.4 2.1 %channel_filter.1 = f32[32,24,128]{2,1,0:T(8,128)S(1)} custom-call(s32[1]{0:T(128)} %bitcast.first_degree, f32[768,128]{1,0:T(8,128)S(1)} %bitcast.2, f32[8,384,384]{2,1,0:T(8,128)S(1)} %copy-done, f32[8,384,384]{2,1,0:T(8,128)S(1)} %copy-done.1), custom_call_target="tpu_custom_call" | custom-call | tf_op jit(solution)/shard_map/channel_filter/pallas_call | solution.py:462
  67.5 15.5 %all_to_all.21.got = f32[32,24,128]{2,1,0:T(8,128)S(1)} all-to-all(f32[32,24,128]{2,1,0:T(8,128)S(1)} %channel_filter.1), channel_id=1, replica_groups=mesh['polar'=4,'azimuth'=8] {'polar','azimuth'}, dimensions={0} | all-to-all | bytes 786432 | tf_op jit(solution)/shard_map/all_to_all | solution.py:476
  83.0 0.0 copy-done.2
  83.0 0.0 copy-done.3
  83.0 0.0 copy-done.11
  83.1 0.0 copy-done.12
  83.1 0.0 copy-start.13
  83.1 0.0 copy-start.7
  83.1 0.0 copy-start.8
  83.1 3.3 %synthesis.1 = f32[32,24,128]{2,1,0:T(8,128)} custom-call(f32[32,24,128]{2,1,0:T(8,128)S(1)} %all_to_all.21.got, f32[24,24,128]{2,1,0:T(8,128)S(1)} %get-tuple-element.8.coef, bf16[128,96]{1,0:T(8,128)(2,1)S(1)} %copy-done.11, bf16[128,96]{1,0:T(8,128)(2,1)S(1)} %copy-done.12, bf16[24,128,256]{2,1,0:T(8,128)(2,1)S(1)} %copy-done.2, ...), custom_call_target="tpu_custom_call" | custom-call | tf_op jit(solution)/shard_map/synthesis/pallas_call | solution.py:478
  86.4 2.6 %all-to-all-start.3 = ((f32[32,24,128]{2,1,0:T(8,128)}), f32[32,24,128]{2,1,0:T(8,128)S(1)}, u32[]{:S(2)}, u32[]{:S(2)}) async-start(f32[32,24,128]{2,1,0:T(8,128)} %synthesis.1), calls=%async_computation.3 | async-start | bytes 786432 | tf_op jit(solution)/shard_map/all_to_all | solution.py:493
  89.0 0.0 copy-done.13
  89.0 13.5 %all-to-all-done.3.got = f32[32,24,128]{2,1,0:T(8,128)S(1)} async-done(((f32[32,24,128]{2,1,0:T(8,128)}), f32[32,24,128]{2,1,0:T(8,128)S(1)}, u32[]{:S(2)}, u32[]{:S(2)}) %all-to-all-start.3) | async-done | bytes 393248 | tf_op jit(solution)/shard_map/all_to_all | solution.py:493
  102.6 0.0 copy-done.7
  102.6 0.0 copy-done.8
  102.6 1.5 %mlp.1 = f32[1,16,12,384]{3,2,1,0:T(8,128)S(1)} custom-call(f32[32,24,128]{2,1,0:T(8,128)S(1)} %all-to-all-done.3.got, f32[1,384]{1,0:T(1,128)S(1)} %reshape.11.gain, bf16[384,768]{1,0:T(8,128)(2,1)S(1)} %copy-done.7, bf16[768,384]{1,0:T(8,128)(2,1)S(1)} %copy-done.8), custom_call_target="tpu_custom_call" | custom-call | tf_op jit(solution)/shard_map/mlp/pallas_call | solution.py:494
  104.1 0.8 copy.15
  (9 shorter events, 0.0 us)
Async XLA Ops:
  0.0 1.3 %copy-start.6 = (f32[1,32,24,384]{3,2,1,0:T(8,128)S(1)}, f32[1,32,24,384]{3,2,1,0:T(8,128)}, u32[]{:S(2)}) copy-start(f32[1,32,24,384]{3,2,1,0:T(8,128)} %field.1) | copy-start | bytes 3538948
  1.3 40.4 %copy-start.5 = (bf16[24,256,128]{2,1,0:T(8,128)(2,1)S(1)}, bf16[24,256,128]{2,1,0:T(8,128)(2,1)}, u32[]{:S(2)}) copy-start(bf16[24,256,128]{2,1,0:T(8,128)(2,1)} %constant.26.clone.leg_low) | copy-start | bytes 4718596
  4.2 37.5 %copy-start.4 = (bf16[24,256,128]{2,1,0:T(8,128)(2,1)S(1)}, bf16[24,256,128]{2,1,0:T(8,128)(2,1)}, u32[]{:S(2)}) copy-start(bf16[24,256,128]{2,1,0:T(8,128)(2,1)} %constant.25.clone.leg_high) | copy-start | bytes 4718596
  4.2 37.5 %copy-start.9 = (bf16[96,192]{1,0:T(8,128)(2,1)S(1)}, bf16[96,192]{1,0:T(8,128)(2,1)}, u32[]{:S(2)}) copy-start(bf16[96,192]{1,0:T(8,128)(2,1)} %constant.23.clone.four_high) | copy-start | bytes 110596
  4.2 37.5 %copy-start.10 = (bf16[96,192]{1,0:T(8,128)(2,1)S(1)}, bf16[96,192]{1,0:T(8,128)(2,1)}, u32[]{:S(2)}) copy-start(bf16[96,192]{1,0:T(8,128)(2,1)} %constant.24.clone.four_low) | copy-start | bytes 110596
  44.6 16.2 %all-to-all-start.1 = ((f32[32,24,128]{2,1,0:T(8,128)}), f32[32,24,128]{2,1,0:T(8,128)S(1)}, u32[]{:S(2)}, u32[]{:S(2)}) async-start(f32[32,24,128]{2,1,0:T(8,128)} %get-tuple-element.7), calls=%async_computation.1 | async-start | bytes 786432 | tf_op jit(solution)/shard_map/all_to_all | solution.py:460
  60.7 2.3 %copy-start = (f32[8,384,384]{2,1,0:T(8,128)S(1)}, f32[8,384,384]{2,1,0:T(8,128)}, u32[]{:S(2)}) copy-start(f32[8,384,384]{2,1,0:T(8,128)} %real.1) | copy-start | bytes 14155780
  63.1 2.3 %copy-start.1 = (f32[8,384,384]{2,1,0:T(8,128)S(1)}, f32[8,384,384]{2,1,0:T(8,128)}, u32[]{:S(2)}) copy-start(f32[8,384,384]{2,1,0:T(8,128)} %imag.1) | copy-start | bytes 14155780
  65.4 17.6 %copy-start.2 = (bf16[24,128,256]{2,1,0:T(8,128)(2,1)S(1)}, bf16[24,128,256]{2,1,0:T(8,128)(2,1)}, u32[]{:S(2)}) copy-start(bf16[24,128,256]{2,1,0:T(8,128)(2,1)} %constant.29.clone.leg_high) | copy-start | bytes 4718596
  65.4 17.6 %copy-start.3 = (bf16[24,128,256]{2,1,0:T(8,128)(2,1)S(1)}, bf16[24,128,256]{2,1,0:T(8,128)(2,1)}, u32[]{:S(2)}) copy-start(bf16[24,128,256]{2,1,0:T(8,128)(2,1)} %constant.30.clone.leg_low) | copy-start | bytes 4718596
  65.4 17.6 %copy-start.11 = (bf16[128,96]{1,0:T(8,128)(2,1)S(1)}, bf16[128,96]{1,0:T(8,128)(2,1)}, u32[]{:S(2)}) copy-start(bf16[128,96]{1,0:T(8,128)(2,1)} %constant.27.clone.four_high) | copy-start | bytes 73732
  65.4 17.6 %copy-start.12 = (bf16[128,96]{1,0:T(8,128)(2,1)S(1)}, bf16[128,96]{1,0:T(8,128)(2,1)}, u32[]{:S(2)}) copy-start(bf16[128,96]{1,0:T(8,128)(2,1)} %constant.28.clone.four_low) | copy-start | bytes 73732
  83.1 6.0 %copy-start.13 = (f32[384]{0:T(512)S(1)}, f32[384]{0:T(512)}, u32[]{:S(2)}) copy-start(f32[384]{0:T(512)} %param.17) | copy-start | bytes 4612
  83.1 19.5 %copy-start.7 = (bf16[384,768]{1,0:T(8,128)(2,1)S(1)}, bf16[384,768]{1,0:T(8,128)(2,1)}, u32[]{:S(2)}) copy-start(bf16[384,768]{1,0:T(8,128)(2,1)} %w_in.1) | copy-start | bytes 1769476
  83.1 19.5 %copy-start.8 = (bf16[768,384]{1,0:T(8,128)(2,1)S(1)}, bf16[768,384]{1,0:T(8,128)(2,1)}, u32[]{:S(2)}) copy-start(bf16[768,384]{1,0:T(8,128)(2,1)} %w_out.1) | copy-start | bytes 1769476
  86.4 16.2 %all-to-all-start.3 = ((f32[32,24,128]{2,1,0:T(8,128)}), f32[32,24,128]{2,1,0:T(8,128)S(1)}, u32[]{:S(2)}, u32[]{:S(2)}) async-start(f32[32,24,128]{2,1,0:T(8,128)} %synthesis.1), calls=%async_computation.3 | async-start | bytes 786432 | tf_op jit(solution)/shard_map/all_to_all | solution.py:493
where the time goes:
time: 105 us
  blocking collectives  53 us (50%)
  waiting for transfers between devices  27.1 us (26%)
  Pallas kernels  12.7 us (12%)
  local copies, waits for them, and re-layouts  6.81 us (6%)
  starting transfers between devices  5.22 us (5%)
    all_to_all x2, blocking collectives, jointly(): got = exchange(sent)  53 us
    all_to_all x2, waiting for transfers between devices, jointly(): got = exchange(sent)  27.1 us
    unnamed x28, local copies, waits for them, and re-layouts  6 us
    all_to_all x2, starting transfers between devices, jointly(): got = exchange(sent)  5.22 us
    pallas_call x1, Pallas kernels, jointly(): pl.pallas_call(functools.partial(synthesis_kernel, polar_count), in_specs...  3.29 us
    pallas_call x1, Pallas kernels, jointly(): pl.pallas_call(scatter_kernel, grid=(lon_cols // 8,), in_specs=[pl.BlockS...  2.89 us
    pallas_call x1, Pallas kernels, jointly(): pl.pallas_call(functools.partial(analysis_kernel, polar_count), in_specs=...  2.84 us
  transfers between devices with their start and end apart: 2, of which 2 were waited for; matrix products, arithmetic and copies ran while one was open for 0% of the time, Pallas kernels for 0%

commit v1 on v0

--- a/solution.py
+++ b/solution.py
@@ -170,24 +170,27 @@
     return 0.5 * values * (1.0 + lax.erf(values * math.sqrt(0.5)))
 
 
-def scatter_kernel(field, sent):
+def scatter_kernel(field, sent, buf, sems):
     devices, rows, channels = sent.shape
-    for tile in range(channels // LANES):
-        lanes = pl.ds(tile * LANES, LANES)
-        blocks = swap([field[0, lat, :, lanes] for lat in range(devices)], OWNER_BITS)
-        for device in range(devices):
-            sent[device, :, lanes] = blocks[device]
+    copies = []
+    for part in range(rows // 8):
+        copy = pltpu.make_async_copy(
+            field.at[0, :, pl.ds(8 * part, 8), :], buf.at[part], sems.at[part]
+        )
+        copy.start()
+        copies.append(copy)
+    for part, copy in enumerate(copies):
+        copy.wait()
+        for tile in range(channels // LANES):
+            lanes = pl.ds(tile * LANES, LANES)
+            blocks = swap([buf[part, lat, :, lanes] for lat in range(devices)], OWNER_BITS)
+            for device in range(devices):
+                sent[device, pl.ds(8 * part, 8), lanes] = blocks[device]
 
 
 def analysis_kernel(
-    polar_count, got, four_high, four_low, leg_high, leg_low, coef, sent, rows, high_buf, low_buf, sems
+    polar_count, got, four_high, four_low, leg_high, leg_low, coef, sent, rows
 ):
-    copies = [
-        pltpu.make_async_copy(leg_high, high_buf, sems.at[0]),
-        pltpu.make_async_copy(leg_low, low_buf, sems.at[1]),
-    ]
-    for copy in copies:
-        copy.start()
     devices, lon_cols, width = got.shape
     azimuth_count = devices // polar_count
     modes = four_high.shape[0]
@@ -204,28 +207,33 @@
             spectra.append(both[:modes] + both[modes:] + dot(four[:modes], block_low))
         for quad, spectrum in enumerate(swap(spectra, QUAD_BITS)):
             rows[pl.ds((tile * polar_count + quad) * modes, modes), :] = spectrum
-    for copy in copies:
-        copy.wait()
-    pairs = orders // 2
     count = 2 * tiles * polar_count
-    for pair in range(pairs):
-        first = rows[pl.ds(pair, count, stride=orders), :]
-        second = rows[pl.ds(pairs + pair, count, stride=orders), :]
-        coef[pair] = dot3(jnp.concatenate([first, second], axis=1), high_buf[pair], low_buf[pair])
+    extra = orders - devices
+    for order in range(devices):
+        first = rows[pl.ds(order, count, stride=orders), :]
+        second = rows[pl.ds(devices + order % extra, count, stride=orders), :]
+        coef[order] = dot3(jnp.concatenate([first, second], axis=1), leg_high[order], leg_low[order])
     pack_by_degree(coef, sent)
 
 
 def pack_by_degree(coef, sent):
-    devices, count, _ = sent.shape
-    pairs = coef.shape[0]
+    devices, count, _ = coef.shape
+    dense, tail = count * 3 // 4, count // 4
+    used = LANES * 3 // 4
     for row in range(0, count, 8):
-        part = pl.ds(row, 8)
-        zero = jnp.zeros((8, LANES), jnp.float32)
-        blocks = swap(
-            [coef[pair, part, :] if pair < pairs else zero for pair in range(devices)], LOW_BITS
-        )
+        blocks = swap([coef[order, pl.ds(row, 8), :] for order in range(devices)], LOW_BITS)
+        head = min(max(dense - row, 0), 8)
         for device in range(devices):
-            sent[device, part, :] = blocks[device]
+            start = device * dense
+            if head:
+                sent[pl.ds(start + row, head), pl.ds(0, used)] = blocks[device][:head, :used]
+            if head < 8:
+                skip = max(row - dense, 0)
+                for part in range(3):
+                    moved = pltpu.roll(blocks[device], used - 32 * part, 1)
+                    sent[pl.ds(start + tail * part + skip, 8 - head), pl.ds(used, LANES - used)] = moved[
+                        head:, used:
+                    ]
 
 
 def filter_kernel(first_degree, got, real, imag, sent, real_buf, imag_buf, turned, sems):
@@ -240,79 +248,114 @@
         for copy in pair:
             copy.start()
         copies.append(pair)
-    devices, count, _ = sent.shape
     tiles = channels // LANES
+    count = 8 * tiles
+    dense, tail = count * 3 // 4, count // 4
+    devices = sent.shape[0] // dense
     groups = [
         (tile, top, quad) for tile in range(tiles) for top in range(2) for quad in range(4)
     ]
+    quarter = lax.broadcasted_iota(jnp.int32, (16, LANES), 1) // 32
     spectra = []
     for half in range(2):
-        parts = [
-            got[pl.ds(top * 16 * count + 2 * (4 * tile + quad) + half, 16, stride=count), :]
-            for tile, top, quad in groups
-        ]
+        parts = []
+        for tile, top, quad in groups:
+            row = 2 * (4 * tile + quad) + half
+            load = lambda start: got[pl.ds(top * 16 * dense + start, 16, stride=dense), :]
+            if row < dense:
+                parts.append(load(row))
+                continue
+            folded = [
+                pltpu.roll(load(tail * part + row - dense), 32 * (part + 1), 1) for part in range(3)
+            ]
+            parts.append(
+                jnp.where(quarter == 0, folded[0], jnp.where(quarter == 1, folded[1], folded[2]))
+            )
         spectra.append(jnp.concatenate(parts, axis=0).T)
-    pad = LANES // (2 * degrees)
-    results = [[None] * (2 * degrees) for _ in range(2)]
+    results = [[None] * 4 for _ in range(2)]
     for degree in range(degrees):
         for copy in copies[degree]:
             copy.wait()
+        places = [(32 * degree, 32), (64 + 16 * degree, 16)]
         own = jnp.concatenate(
-            [
-                spectra[half][(order * degrees + degree) * pad : (order * degrees + degree + 1) * pad]
-                for half in range(2)
-                for order in range(2)
-            ],
+            [spectra[half][start : start + size] for half in range(2) for start, size in places],
             axis=0,
         )
         by_real = dot3(own, *split_bf16(real_buf[degree]))
         by_imag = dot3(own, *split_bf16(imag_buf[degree]))
-        size = 2 * pad
-        out_re = by_real[:size] - by_imag[size:]
-        out_im = by_real[size:] + by_imag[:size]
-        for order in range(2):
-            results[0][order * degrees + degree] = out_re[order * pad : (order + 1) * pad]
-            results[1][order * degrees + degree] = out_im[order * pad : (order + 1) * pad]
+        size = 48
+        outs = (by_real[:size] - by_imag[size:], by_real[size:] + by_imag[:size])
+        for half in range(2):
+            results[half][degree] = outs[half][:32]
+            results[half][2 + degree] = outs[half][32:]
+    across = []
     for half in range(2):
-        across = jnp.concatenate(results[half], axis=0).T
-        for place, (tile, top, quad) in enumerate(groups):
-            turned[pl.ds(((top * tiles * 4 + 4 * tile + quad) * 2 + half) * 16, 16), :] = across[
-                place * 16 : (place + 1) * 16
-            ]
+        padding = jnp.zeros((32, channels), jnp.float32)
+        across.append(jnp.concatenate(results[half] + [padding], axis=0).T)
+    for top in range(2):
+        rows = []
+        for row in range(count):
+            tile, quad, half = row // 8, row // 2 % 4, row % 2
+            start = ((tile * 2 + top) * 4 + quad) * 16
+            rows.append(across[half][start : start + 16])
+        for row in range(dense):
+            part = row // tail
+            folded = pltpu.roll(rows[dense + row % tail], 96 - 32 * part, 1)
+            turned[pl.ds((top * dense + row) * 16, 16), :] = jnp.where(
+                quarter < 3, rows[row], folded
+            )
     for device in range(devices):
-        sent[device] = turned[pl.ds(device // 16 * 16 * count + device % 16, count, stride=16), :]
+        sent[pl.ds(device * dense, dense), :] = turned[
+            pl.ds(device // 16 * 16 * dense + device % 16, dense, stride=16), :
+        ]
 
 
 def synthesis_kernel(
-    polar_count, got, coef, four_high, four_low, leg_high, leg_low, sent, back, modes_buf,
-    high_buf, low_buf, sems
+    polar_count, got, coef, four_high, four_low, leg_high, leg_low, sent, tails, back, modes_buf
 ):
-    copies = [
-        pltpu.make_async_copy(leg_high, high_buf, sems.at[0]),
-        pltpu.make_async_copy(leg_low, low_buf, sems.at[1]),
-    ]
-    for copy in copies:
-        copy.start()
-    devices, count, _ = got.shape
+    devices, count, _ = coef.shape
+    dense, tail = count * 3 // 4, count // 4
     azimuth_count = devices // polar_count
-    pairs = coef.shape[0]
-    orders = 2 * pairs
+    orders = four_high.shape[1] // 2
+    extra = orders - devices
+    quarter = lax.broadcasted_iota(jnp.int32, (tail, LANES), 1) // 32
+    for device in range(devices):
+        folded = [
+            pltpu.roll(got[pl.ds(device * dense + tail * part, tail), :], 32 * (part + 1), 1)
+            for part in range(3)
+        ]
+        tails[device, pl.ds(8 - tail, tail), :] = jnp.where(
+            quarter == 0, folded[0], jnp.where(quarter == 1, folded[1], folded[2])
+        )
+        tails[device, pl.ds(0, 8 - tail), :] = got[
+            pl.ds(device * dense + count - 8, 8 - tail), :
+        ]
     for row in range(0, count, 8):
-        part = pl.ds(row, 8)
-        blocks = swap([got[device, part, :] for device in range(devices)], LOW_BITS)
-        for pair in range(pairs):
-            back[pair, part, :] = blocks[pair]
-    for copy in copies:
-        copy.wait()
+        if row + 8 < count:
+            blocks = [got[pl.ds(device * dense + row, 8), :] for device in range(devices)]
+        else:
+            blocks = [tails[device] for device in range(devices)]
+        blocks = swap(blocks, LOW_BITS)
+        for order in range(devices):
+            back[order, pl.ds(row, 8), :] = blocks[order]
     keep = (lax.broadcasted_iota(jnp.int32, (count, LANES), 1) & 64) == 0
-    for pair in range(pairs):
-        both = jnp.concatenate([coef[pair], back[pair]], axis=0)
-        values = dot3(both, high_buf[pair], low_buf[pair])
-        for order in range(2):
-            lanes = slice(order * LANES, (order + 1) * LANES)
-            modes_buf[pl.ds((order * pairs + pair) * count, count), :] = jnp.where(
-                keep, values[:count, lanes], values[count:, lanes]
+    for order in range(devices):
+        both = jnp.concatenate([coef[order], back[order]], axis=0)
+        values = dot3(both, leg_high[order], leg_low[order])
+        merged = [
+            jnp.where(
+                keep,
+                values[:count, part * LANES : (part + 1) * LANES],
+                values[count:, part * LANES : (part + 1) * LANES],
             )
+            for part in range(2)
+        ]
+        modes_buf[pl.ds(order * count, count), :] = merged[0]
+        later = devices + order % extra
+        if order < extra:
+            modes_buf[pl.ds(later * count, count), :] = merged[1]
+        else:
+            modes_buf[pl.ds(later * count, count), :] += merged[1]
     four = jnp.concatenate([four_high[...], four_low[...]], axis=0)
     points = four_high.shape[0]
     half = points // 2
@@ -333,30 +376,41 @@
             states.append(gelu(branch) + skip)
         for polar, state in enumerate(swap(states, QUAD_BITS)):
             for azimuth in range(azimuth_count):
-                sent[polar * azimuth_count + azimuth, pl.ds(8 * tile, 8), :] = state[
-                    8 * azimuth : 8 * azimuth + 8
+                device = polar * azimuth_count + azimuth
+                sent[pl.ds(device * dense + tail * tile, tail), :] = state[
+                    tail * azimuth : tail * (azimuth + 1)
                 ]
 
 
-def mlp_kernel(got, gain, w_in, w_out, mixed, state):
-    devices, count, _ = got.shape
-    tiles = count // 8
+def mlp_kernel(got, gain, w_in, w_out, mixed, state, result, sem):
+    channels = state.shape[1]
+    _, lat_rows, lon_cols, _ = mixed.shape
+    part = lon_cols // 2
+    tiles = channels // LANES
+    devices = got.shape[0] // (tiles * part)
     for tile in range(tiles):
-        blocks = swap([got[device, pl.ds(8 * tile, 8), :] for device in range(devices)], OWNER_BITS)
+        blocks = swap(
+            [
+                got[pl.ds((device * tiles + tile) * part, part), :]
+                for device in range(devices)
+            ],
+            OWNER_BITS,
+        )
         for device in range(devices):
-            state[pl.ds(8 * device, 8), pl.ds(tile * LANES, LANES)] = blocks[device]
+            state[pl.ds(part * device, part), pl.ds(tile * LANES, LANES)] = blocks[device]
     value = state[...]
     center = jnp.mean(value, axis=-1, keepdims=True)
     spread = jnp.mean((value - center) ** 2, axis=-1, keepdims=True)
     normed = ((value - center) * lax.rsqrt(spread + 1e-05) * gain[...]).astype(jnp.bfloat16)
     hidden = gelu(dot(normed, w_in[...])).astype(jnp.bfloat16)
     state[...] = value + dot(hidden, w_out[...])
-    _, lat_rows, lon_cols, _ = mixed.shape
-    part = lon_cols // 2
     for top in range(2):
         for lat in range(lat_rows):
-            row = 8 * (top * lat_rows + lat)
-            mixed[0, lat, pl.ds(top * part, part), :] = state[pl.ds(row, part), :]
+            row = part * (top * lat_rows + lat)
+            result[0, lat, pl.ds(top * part, part), :] = state[pl.ds(row, part), :]
+    copy = pltpu.make_async_copy(result, mixed, sem)
+    copy.start()
+    copy.wait()
 
 
 def joint_fits(field, filter_real, polar_count, azimuth_count):
@@ -368,12 +422,10 @@
         and devices == 32
         and polar_count == 4
         and lat_rows == 32
-        and lon_cols % 8 == 0
-        and lon_cols // 4 <= 8
-        and channels % LANES == 0
+        and lon_cols == 24
+        and channels == 3 * LANES
         and filter_real.shape[0] == 2 * polar_count
-        and orders % 16 == 0
-        and orders // 2 <= 32
+        and 2 * orders == 3 * devices
     )
 
 
@@ -385,8 +437,7 @@
     fine_lat, fine_lon = lat_rows * polar_count, lon_cols * azimuth_count
     coarse_lat, coarse_lon = fine_lat // 2, fine_lon // 2
     orders = coarse_lon // 2
-    pairs = orders // 2
-    tiles = channels // LANES
+    extra = orders - devices
     count = 2 * channels // devices
     degrees_here = coarse_lat // devices
     lat_out, lon_out = coarse_lat // polar_count, coarse_lon // azimuth_count
@@ -396,11 +447,8 @@
     forward = fourier_table(fine_lon, mode_ids, halves, np.ones(2 * orders)).T
     twofold = np.where(mode_ids == 0, 1.0, 2.0)
     inverse = fourier_table(coarse_lon, mode_ids, halves, twofold)
-    backward = np.zeros((2, azimuth_count, 8, 2 * orders))
-    backward[:, :, : lon_out // 2] = inverse.reshape(
-        azimuth_count, 2, lon_out // 2, 2 * orders
-    ).transpose(1, 0, 2, 3)
-    backward = backward.reshape(-1, 2 * orders)
+    backward = inverse.reshape(azimuth_count, 2, lon_out // 2, 2 * orders)
+    backward = backward.transpose(1, 0, 2, 3).reshape(-1, 2 * orders)
 
     fine_nodes = colatitudes(fine_lat)
     quadrature = math.pi / fine_lat * np.sin(fine_nodes) * (2.0 * math.pi / fine_lon)
@@ -416,90 +464,101 @@
     lat_coarse = (lane >> 4 & 3) * lat_out + (lane & 15)
     fine = fine[:, degree][:, :, lat_fine].transpose(0, 2, 1)
     coarse = coarse[:, degree][:, :, lat_coarse]
-    size = degree.shape[0]
-    analyse = np.zeros((pairs, 2, LANES, 2, size))
-    synthesise = np.zeros((pairs, 2, size, 2, LANES))
-    for order in range(2):
-        analyse[:, order, :, order, :] = fine[order * pairs : (order + 1) * pairs]
-        synthesise[:, order, :, order, :] = coarse[order * pairs : (order + 1) * pairs]
-    analyse = analyse.reshape(pairs, 2 * LANES, 2 * size)
-    synthesise = synthesise.reshape(pairs, 2 * size, 2 * LANES)
+    analyse = np.zeros((devices, 2, LANES, 4, devices))
+    synthesise = np.zeros((devices, 4, devices, 2, LANES))
+    for order in range(devices):
+        later, which = devices + order % extra, order // extra
+        own = slice(which * devices, (which + 1) * devices)
+        analyse[order, 0, :, :2] = fine[order].reshape(LANES, 2, devices)
+        analyse[order, 1, :, 2] = fine[later][:, own]
+        synthesise[order, :2, :, 0] = coarse[order].reshape(2, devices, LANES)
+        synthesise[order, 2, :, 1] = coarse[later][own]
+    analyse = analyse.reshape(devices, 2 * LANES, LANES)
+    synthesise = synthesise.reshape(devices, LANES, 2 * LANES)
 
     vmem = pl.BlockSpec(memory_space=pltpu.VMEM)
-    anywhere = pl.BlockSpec(memory_space=pl.ANY)
-    block = jax.ShapeDtypeStruct((devices, count, LANES), jnp.float32)
-    exchange = functools.partial(
-        lax.all_to_all, axis_name=BOTH, split_axis=0, concat_axis=0, tiled=True
-    )
+    hbm = pl.BlockSpec(memory_space=pltpu.HBM)
+    dense = count * 3 // 4
+    block = pltpu.VMEM((devices * dense, LANES), jnp.float32)
+
+    def exchange(blocks):
+        split = blocks.reshape((devices, -1, 2, LANES)) if blocks.ndim == 2 else blocks
+        moved = lax.all_to_all(split, BOTH, split_axis=0, concat_axis=0, tiled=True)
+        return moved.reshape(blocks.shape)
+
+    def near(*arrays):
+        return [pltpu.with_memory_space_constraint(array, pltpu.VMEM) for array in arrays]
+
+    def far(*arrays):
+        return [pltpu.with_memory_space_constraint(array, pltpu.HBM) for array in arrays]
 
     sent = pl.pallas_call(
         scatter_kernel,
-        grid=(lon_cols // 8,),
-        in_specs=[pl.BlockSpec((1, lat_rows, 8, channels), lambda step: (0, 0, step, 0))],
-        out_specs=pl.BlockSpec((devices, 8, channels), lambda step: (0, step, 0)),
-        out_shape=jax.ShapeDtypeStruct((devices, lon_cols, channels), jnp.float32),
+        in_specs=[hbm],
+        out_specs=vmem,
+        out_shape=pltpu.VMEM((devices, lon_cols, channels), jnp.float32),
+        scratch_shapes=[
+            pltpu.VMEM((lon_cols // 8, lat_rows, 8, channels), jnp.float32),
+            pltpu.SemaphoreType.DMA((lon_cols // 8,)),
+        ],
         compiler_params=pltpu.CompilerParams(vmem_limit_bytes=8 * MIB),
         name="scatter_channels",
-    )(field)
+    )(*far(field))
     got = exchange(sent)
-    table_buf = pltpu.VMEM(analyse.shape, jnp.bfloat16)
     coef, sent = pl.pallas_call(
         functools.partial(analysis_kernel, polar_count),
-        in_specs=[vmem, vmem, vmem, anywhere, anywhere],
+        in_specs=[vmem] * 5,
         out_specs=[vmem, vmem],
-        out_shape=[jax.ShapeDtypeStruct((pairs, count, LANES), jnp.float32), block],
-        scratch_shapes=[
-            pltpu.VMEM((count * orders, LANES), jnp.float32),
-            table_buf,
-            table_buf,
-            pltpu.SemaphoreType.DMA((2,)),
-        ],
-        compiler_params=pltpu.CompilerParams(vmem_limit_bytes=16 * MIB),
+        out_shape=[pltpu.VMEM((devices, count, LANES), jnp.float32), block],
+        scratch_shapes=[pltpu.VMEM((count * orders, LANES), jnp.float32)],
+        compiler_params=pltpu.CompilerParams(vmem_limit_bytes=8 * MIB),
         name="analysis",
-    )(got, *split_constant(forward), *split_constant(analyse))
+    )(*near(got, *split_constant(forward), *split_constant(analyse)))
     got = exchange(sent)
     first_degree = (lax.axis_index("polar") * degrees_here).astype(jnp.int32).reshape(1)
     sent = pl.pallas_call(
         filter_kernel,
-        in_specs=[pl.BlockSpec(memory_space=pltpu.SMEM), vmem, anywhere, anywhere],
+        in_specs=[pl.BlockSpec(memory_space=pltpu.SMEM), vmem, hbm, hbm],
         out_specs=vmem,
         out_shape=block,
         scratch_shapes=[
             pltpu.VMEM((degrees_here, channels, channels), jnp.float32),
             pltpu.VMEM((degrees_here, channels, channels), jnp.float32),
-            pltpu.VMEM((2 * channels, LANES), jnp.float32),
+            pltpu.VMEM((devices * dense, LANES), jnp.float32),
             pltpu.SemaphoreType.DMA((2, degrees_here)),
         ],
-        compiler_params=pltpu.CompilerParams(vmem_limit_bytes=16 * MIB),
+        compiler_params=pltpu.CompilerParams(vmem_limit_bytes=8 * MIB),
         name="channel_filter",
-    )(first_degree, got.reshape(devices * count, LANES), filter_real, filter_imag)
+    )(first_degree, *near(got), *far(filter_real, filter_imag))
     got = exchange(sent)
-    table_buf = pltpu.VMEM(synthesise.shape, jnp.bfloat16)
     sent = pl.pallas_call(
         functools.partial(synthesis_kernel, polar_count),
-        in_specs=[vmem, vmem, vmem, vmem, anywhere, anywhere],
+        in_specs=[vmem] * 6,
         out_specs=vmem,
         out_shape=block,
         scratch_shapes=[
-            pltpu.VMEM((pairs, count, LANES), jnp.float32),
+            pltpu.VMEM((devices, 8, LANES), jnp.float32),
+            pltpu.VMEM((devices, count, LANES), jnp.float32),
             pltpu.VMEM((orders * count, LANES), jnp.float32),
-            table_buf,
-            table_buf,
-            pltpu.SemaphoreType.DMA((2,)),
         ],
-        compiler_params=pltpu.CompilerParams(vmem_limit_bytes=16 * MIB),
+        compiler_params=pltpu.CompilerParams(vmem_limit_bytes=8 * MIB),
         name="synthesis",
-    )(got, coef, *split_constant(backward), *split_constant(synthesise))
+    )(*near(got, coef, *split_constant(backward), *split_constant(synthesise)))
     got = exchange(sent)
+    result = (1, lat_out, lon_out, channels)
     return pl.pallas_call(
         mlp_kernel,
         in_specs=[vmem] * 4,
-        out_specs=vmem,
-        out_shape=jax.ShapeDtypeStruct((1, lat_out, lon_out, channels), jnp.float32),
-        scratch_shapes=[pltpu.VMEM((8 * devices, channels), jnp.float32)],
-        compiler_params=pltpu.CompilerParams(vmem_limit_bytes=16 * MIB),
+        out_specs=pl.BlockSpec(memory_space=pl.ANY),
+        out_shape=jax.ShapeDtypeStruct(result, jnp.float32),
+        scratch_shapes=[
+            pltpu.VMEM((lat_out * lon_out, channels), jnp.float32),
+            pltpu.VMEM(result, jnp.float32),
+            pltpu.SemaphoreType.DMA,
+        ],
+        compiler_params=pltpu.CompilerParams(vmem_limit_bytes=8 * MIB),
         name="mlp",
-    )(got, norm_gain.reshape(1, channels), w_in, w_out)
+    )(*near(got, norm_gain.reshape(1, channels), w_in, w_out))
 
 
 def per_device(field, filter_real, filter_imag, norm_gain, w_in, w_out):

time: 105 us -> 94.3 us (0.90)
  local copies, waits for them, and re-layouts: 6.81 us -> 0.86 us
  waiting for transfers between devices: 27.1 us -> 22.8 us
  blocking collectives: 53 us -> 50.9 us
  Pallas kernels: 12.7 us -> 14 us
    unnamed x28 -> x22, local copies, waits for them, and re-layouts: 6 us -> 0.05 us
    all_to_all x2, waiting for transfers between devices: 27.1 us -> 22.8 us  [exchange(): moved = lax.all_to_all(split, BOTH, split_axis=0, concat_axis=0, tiled=True)]
    all_to_all x2, blocking collectives: 53 us -> 50.9 us  [exchange(): moved = lax.all_to_all(split, BOTH, split_axis=0, concat_axis=0, tiled=True)]
    pallas_call x2, Pallas kernels: 4.43 us -> 5.51 us  [the longest x1 3.97 us: jointly(): pl.pallas_call(scatter_kernel, in_specs=[hbm], out_specs=vmem, out_shape=...]
where the time goes in v1:
time: 94.3 us; the launch traced here: 94 us
  blocking collectives  50.9 us (54%)
  waiting for transfers between devices  22.8 us (24%)
  Pallas kernels  14 us (15%)
  starting transfers between devices  5.18 us (5%)
    all_to_all x2, blocking collectives, exchange(): moved = lax.all_to_all(split, BOTH, split_axis=0, concat_axis=0, tiled=True)  50.9 us
    all_to_all x2, waiting for transfers between devices, exchange(): moved = lax.all_to_all(split, BOTH, split_axis=0, concat_axis=0, tiled=True)  22.8 us
    all_to_all x2, starting transfers between devices, exchange(): moved = lax.all_to_all(split, BOTH, split_axis=0, concat_axis=0, tiled=True)  5.18 us
    pallas_call x1, Pallas kernels, jointly(): pl.pallas_call(scatter_kernel, in_specs=[hbm], out_specs=vmem, out_shape=...  3.97 us
    pallas_call x1, Pallas kernels, jointly(): pl.pallas_call(functools.partial(synthesis_kernel, polar_count), in_specs...  2.95 us
    pallas_call x1, Pallas kernels, jointly(): pl.pallas_call(functools.partial(analysis_kernel, polar_count), in_specs=...  2.89 us
    pallas_call x1, Pallas kernels, jointly(): pl.pallas_call(filter_kernel, in_specs=[pl.BlockSpec(memory_space=pltpu.S...  2.69 us
  transfers between devices with their start and end apart: 2, of which 2 were waited for; matrix products, arithmetic and copies ran while one was open for 0% of the time, Pallas kernels for 0%

profile of v1, /device:TPU:0, one launch (start us, length us, event | category | flops | bytes accessed | tf_op | source)
XLA Modules:
  0.0 94.0 jit_solution(3878180568369175094)
XLA Ops:
  0.0 0.0 copy-start.3
  0.0 0.0 copy-start.6
  0.0 0.0 copy-start.7
  0.0 4.0 %scatter_channels.1 = f32[32,24,384]{2,1,0:T(8,128)S(1)} custom-call(f32[1,32,24,384]{3,2,1,0:T(8,128)} %field.1), custom_call_target="tpu_custom_call" | custom-call | tf_op jit(solution)/shard_map/scatter_channels/pallas_call | solution.py:495
  4.0 37.5 %all_to_all.20.got = f32[32,24,384]{2,1,0:T(8,128)S(1)} all-to-all(f32[32,24,384]{2,1,0:T(8,128)S(1)} %scatter_channels.1), channel_id=1, replica_groups=mesh['polar'=4,'azimuth'=8] {'polar','azimuth'}, dimensions={0} | all-to-all | bytes 2359296 | tf_op jit(solution)/shard_map/all_to_all | solution.py:486
  41.5 0.0 copy-done.2
  41.5 0.0 copy-done.3
  41.5 0.0 copy-done.6
  41.5 0.0 copy-done.7
  41.5 2.9 %analysis.1 = (f32[32,24,128]{2,1,0:T(8,128)S(1)}, f32[576,128]{1,0:T(8,128)}) custom-call(f32[32,24,384]{2,1,0:T(8,128)S(1)} %all_to_all.20.got, bf16[96,192]{1,0:T(8,128)(2,1)S(1)} %copy-done.6, bf16[96,192]{1,0:T(8,128)(2,1)S(1)} %copy-done.7, bf16[32,256,128]{2,1,0:T(8,128)(2,1)S(1)} %copy-done.2, bf16[32,256,128]{2,1,0:T(8,128)(2,1)S(1)} %copy-done.3), custom_call_target="tpu_custom_call" | custom-call | tf_op jit(solution)/shard_map/analysis/pallas_call | solution.py:508
  44.4 2.6 %all-to-all-start.1 = ((f32[32,9,2,128]{3,2,1,0:T(2,128)}), f32[32,9,2,128]{3,2,1,0:T(2,128)S(1)}, u32[]{:S(2)}, u32[]{:S(2)}) async-start(f32[32,9,2,128]{3,2,1,0:T(2,128)} %bitcast.1), calls=%async_computation.1 | async-start | bytes 589824 | tf_op jit(solution)/shard_map/all_to_all | solution.py:486
  47.0 11.4 %all-to-all-done.1 = f32[32,9,2,128]{3,2,1,0:T(2,128)S(1)} async-done(((f32[32,9,2,128]{3,2,1,0:T(2,128)}), f32[32,9,2,128]{3,2,1,0:T(2,128)S(1)}, u32[]{:S(2)}, u32[]{:S(2)}) %all-to-all-start.1) | async-done | bytes 294944 | tf_op jit(solution)/shard_map/all_to_all | solution.py:486
  58.5 0.0 copy-start
  58.5 0.0 copy-start.1
  58.5 0.0 copy-start.8
  58.5 2.7 %channel_filter.1 = f32[576,128]{1,0:T(8,128)S(1)} custom-call(s32[1]{0:T(128)} %bitcast.first_degree, f32[576,128]{1,0:T(8,128)S(1)} %bitcast.7, f32[8,384,384]{2,1,0:T(8,128)} %real.1, f32[8,384,384]{2,1,0:T(8,128)} %imag.1), custom_call_target="tpu_custom_call" | custom-call | tf_op jit(solution)/shard_map/channel_filter/pallas_call | solution.py:519
  61.2 13.4 %all_to_all.21 = f32[32,9,2,128]{3,2,1,0:T(2,128)S(1)} all-to-all(f32[32,9,2,128]{3,2,1,0:T(2,128)S(1)} %bitcast.9), channel_id=1, replica_groups=mesh['polar'=4,'azimuth'=8] {'polar','azimuth'}, dimensions={0} | all-to-all | bytes 589824 | tf_op jit(solution)/shard_map/all_to_all | solution.py:486
  74.6 0.0 copy-done
  74.6 0.0 copy-done.1
  74.6 0.0 copy-done.8
  74.6 0.0 copy-done.9
  74.6 0.0 copy-start.10
  74.6 0.0 copy-start.4
  74.6 0.0 copy-start.5
  74.6 3.0 %synthesis.1 = f32[576,128]{1,0:T(8,128)} custom-call(f32[576,128]{1,0:T(8,128)S(1)} %bitcast.8, f32[32,24,128]{2,1,0:T(8,128)S(1)} %get-tuple-element.8.coef, bf16[96,96]{1,0:T(8,128)(2,1)S(1)} %copy-done.8, bf16[96,96]{1,0:T(8,128)(2,1)S(1)} %copy-done.9, bf16[32,128,256]{2,1,0:T(8,128)(2,1)S(1)} %copy-done, bf16[32,128,256]{2,1,0:T(8,128)(2,1)S(1)} %copy-done.1), custom_call_target="tpu_custom_call" | custom-call | tf_op jit(solution)/shard_map/synthesis/pallas_call | solution.py:534
  77.6 2.6 %all-to-all-start.3 = ((f32[32,9,2,128]{3,2,1,0:T(2,128)}), f32[32,9,2,128]{3,2,1,0:T(2,128)S(1)}, u32[]{:S(2)}, u32[]{:S(2)}) async-start(f32[32,9,2,128]{3,2,1,0:T(2,128)} %bitcast.5), calls=%async_computation.3 | async-start | bytes 589824 | tf_op jit(solution)/shard_map/all_to_all | solution.py:486
  80.2 0.0 copy-done.10
  80.2 11.4 %all-to-all-done.3 = f32[32,9,2,128]{3,2,1,0:T(2,128)S(1)} async-done(((f32[32,9,2,128]{3,2,1,0:T(2,128)}), f32[32,9,2,128]{3,2,1,0:T(2,128)S(1)}, u32[]{:S(2)}, u32[]{:S(2)}) %all-to-all-start.3) | async-done | bytes 294944 | tf_op jit(solution)/shard_map/all_to_all | solution.py:486
  91.6 0.0 copy-done.4
  91.6 0.0 copy-done.5
  91.6 1.5 %mlp.1 = f32[1,16,12,384]{3,2,1,0:T(8,128)S(1)} custom-call(f32[576,128]{1,0:T(8,128)S(1)} %bitcast.10, f32[1,384]{1,0:T(1,128)S(1)} %reshape.31.gain, bf16[384,768]{1,0:T(8,128)(2,1)S(1)} %copy-done.4, bf16[768,384]{1,0:T(8,128)(2,1)S(1)} %copy-done.5), custom_call_target="tpu_custom_call" | custom-call | tf_op jit(solution)/shard_map/mlp/pallas_call | solution.py:549
  93.2 0.8 copy.15
  (3 shorter events, 0.0 us)
Async XLA Ops:
  0.0 41.5 %copy-start.2 = (bf16[32,256,128]{2,1,0:T(8,128)(2,1)S(1)}, bf16[32,256,128]{2,1,0:T(8,128)(2,1)}, u32[]{:S(2)}) copy-start(bf16[32,256,128]{2,1,0:T(8,128)(2,1)} %constant.25.clone.leg_high) | copy-start | bytes 6291460
  0.0 41.5 %copy-start.3 = (bf16[32,256,128]{2,1,0:T(8,128)(2,1)S(1)}, bf16[32,256,128]{2,1,0:T(8,128)(2,1)}, u32[]{:S(2)}) copy-start(bf16[32,256,128]{2,1,0:T(8,128)(2,1)} %constant.26.clone.leg_low) | copy-start | bytes 6291460
  0.0 41.5 %copy-start.6 = (bf16[96,192]{1,0:T(8,128)(2,1)S(1)}, bf16[96,192]{1,0:T(8,128)(2,1)}, u32[]{:S(2)}) copy-start(bf16[96,192]{1,0:T(8,128)(2,1)} %constant.23.clone.four_high) | copy-start | bytes 110596
  0.0 41.5 %copy-start.7 = (bf16[96,192]{1,0:T(8,128)(2,1)S(1)}, bf16[96,192]{1,0:T(8,128)(2,1)}, u32[]{:S(2)}) copy-start(bf16[96,192]{1,0:T(8,128)(2,1)} %constant.24.clone.four_low) | copy-start | bytes 110596
  44.4 14.0 %all-to-all-start.1 = ((f32[32,9,2,128]{3,2,1,0:T(2,128)}), f32[32,9,2,128]{3,2,1,0:T(2,128)S(1)}, u32[]{:S(2)}, u32[]{:S(2)}) async-start(f32[32,9,2,128]{3,2,1,0:T(2,128)} %bitcast.1), calls=%async_computation.1 | async-start | bytes 589824 | tf_op jit(solution)/shard_map/all_to_all | solution.py:486
  58.5 16.1 %copy-start = (bf16[32,128,256]{2,1,0:T(8,128)(2,1)S(1)}, bf16[32,128,256]{2,1,0:T(8,128)(2,1)}, u32[]{:S(2)}) copy-start(bf16[32,128,256]{2,1,0:T(8,128)(2,1)} %constant.29.clone.leg_high) | copy-start | bytes 6291460
  58.5 16.1 %copy-start.1 = (bf16[32,128,256]{2,1,0:T(8,128)(2,1)S(1)}, bf16[32,128,256]{2,1,0:T(8,128)(2,1)}, u32[]{:S(2)}) copy-start(bf16[32,128,256]{2,1,0:T(8,128)(2,1)} %constant.30.clone.leg_low) | copy-start | bytes 6291460
  58.5 16.1 %copy-start.8 = (bf16[96,96]{1,0:T(8,128)(2,1)S(1)}, bf16[96,96]{1,0:T(8,128)(2,1)}, u32[]{:S(2)}) copy-start(bf16[96,96]{1,0:T(8,128)(2,1)} %constant.27.clone.four_high) | copy-start | bytes 55300
  58.5 16.1 %copy-start.9 = (bf16[96,96]{1,0:T(8,128)(2,1)S(1)}, bf16[96,96]{1,0:T(8,128)(2,1)}, u32[]{:S(2)}) copy-start(bf16[96,96]{1,0:T(8,128)(2,1)} %constant.28.clone.four_low) | copy-start | bytes 55300
  74.6 5.6 %copy-start.10 = (f32[384]{0:T(512)S(1)}, f32[384]{0:T(512)}, u32[]{:S(2)}) copy-start(f32[384]{0:T(512)} %param.17) | copy-start | bytes 4612
  74.6 17.0 %copy-start.4 = (bf16[384,768]{1,0:T(8,128)(2,1)S(1)}, bf16[384,768]{1,0:T(8,128)(2,1)}, u32[]{:S(2)}) copy-start(bf16[384,768]{1,0:T(8,128)(2,1)} %w_in.1) | copy-start | bytes 1769476
  74.6 17.0 %copy-start.5 = (bf16[768,384]{1,0:T(8,128)(2,1)S(1)}, bf16[768,384]{1,0:T(8,128)(2,1)}, u32[]{:S(2)}) copy-start(bf16[768,384]{1,0:T(8,128)(2,1)} %w_out.1) | copy-start | bytes 1769476
  77.6 14.0 %all-to-all-start.3 = ((f32[32,9,2,128]{3,2,1,0:T(2,128)}), f32[32,9,2,128]{3,2,1,0:T(2,128)S(1)}, u32[]{:S(2)}, u32[]{:S(2)}) async-start(f32[32,9,2,128]{3,2,1,0:T(2,128)} %bitcast.5), calls=%async_computation.3 | async-start | bytes 589824 | tf_op jit(solution)/shard_map/all_to_all | solution.py:486

commit v2 on v1

--- a/solution.py
+++ b/solution.py
@@ -143,49 +143,61 @@
     return both[:rows] + both[rows:] + dot(left_high, right_low)
 
 
-def swap(blocks, bits):
-    lane = lax.broadcasted_iota(jnp.int32, blocks[0].shape, len(blocks[0].shape) - 1)
+def swap(blocks, step):
+    count = len(blocks)
     axis = len(blocks[0].shape) - 1
-    blocks = list(blocks)
-    for order, bit in enumerate(bits):
-        step = 1 << bit
-        keep = (lane & step) == 0
-        for index in range(len(blocks)):
-            if index >> order & 1:
-                continue
-            first, second = blocks[index], blocks[index | 1 << order]
-            blocks[index] = jnp.where(keep, first, pltpu.roll(second, step, axis))
-            blocks[index | 1 << order] = jnp.where(
-                keep, pltpu.roll(first, LANES - step, axis), second
-            )
-    return blocks
-
-
-OWNER_BITS = (0, 1, 2, 3, 6)
-QUAD_BITS = (4, 5)
-LOW_BITS = (0, 1, 2, 3, 4)
+    turn = lambda block, fields: (
+        pltpu.roll(block, fields * step % LANES, axis) if fields * step % LANES else block
+    )
+    place = lax.broadcasted_iota(jnp.int32, blocks[0].shape, axis) // step
+    turned = [turn(blocks[-index % count], -index % count) for index in range(count)]
+    shift = 1
+    while shift < count:
+        take = (place & shift) != 0
+        turned = [
+            jnp.where(take, turned[(index - shift) % count], turned[index]) for index in range(count)
+        ]
+        shift *= 2
+    return [turn(block, -index) for index, block in enumerate(turned)]
+
+
+QUAD = 4
+FIELD = LANES // QUAD
 
 
 def gelu(values):
     return 0.5 * values * (1.0 + lax.erf(values * math.sqrt(0.5)))
 
 
-def scatter_kernel(field, sent, buf, sems):
+def scatter_kernel(field, real, imag, sent, own_filter, buf, sems, filter_sems):
     devices, rows, channels = sent.shape
+    parts = [(row, tile) for row in range(rows // 8) for tile in range(channels // LANES)]
     copies = []
-    for part in range(rows // 8):
+    for index, (row, tile) in enumerate(parts):
         copy = pltpu.make_async_copy(
-            field.at[0, :, pl.ds(8 * part, 8), :], buf.at[part], sems.at[part]
+            field.at[0, :, pl.ds(8 * row, 8), pl.ds(tile * LANES, LANES)],
+            buf.at[index],
+            sems.at[index],
         )
         copy.start()
         copies.append(copy)
-    for part, copy in enumerate(copies):
+    degrees = own_filter.shape[1]
+    start = lax.axis_index("polar") * degrees
+    filter_copies = [
+        pltpu.make_async_copy(
+            part.at[pl.ds(start, degrees)], own_filter.at[index], filter_sems.at[index]
+        )
+        for index, part in enumerate((real, imag))
+    ]
+    for copy in filter_copies:
+        copy.start()
+    for index, (row, tile) in enumerate(parts):
+        copies[index].wait()
+        blocks = swap([buf[index, lat] for lat in range(devices)], 1)
+        for device in range(devices):
+            sent[device, pl.ds(8 * row, 8), pl.ds(tile * LANES, LANES)] = blocks[device]
+    for copy in filter_copies:
         copy.wait()
-        for tile in range(channels // LANES):
-            lanes = pl.ds(tile * LANES, LANES)
-            blocks = swap([buf[part, lat, :, lanes] for lat in range(devices)], OWNER_BITS)
-            for device in range(devices):
-                sent[device, pl.ds(8 * part, 8), lanes] = blocks[device]
 
 
 def analysis_kernel(
@@ -197,15 +209,15 @@
     orders = modes // 2
     four = jnp.concatenate([four_high[...], four_low[...]], axis=0)
     tiles = width // LANES
+    wide = []
+    for polar in range(polar_count):
+        block = got[pl.ds(polar * azimuth_count, azimuth_count)]
+        block_high, block_low = split_bf16(block.reshape(azimuth_count * lon_cols, width))
+        both = dot(four, block_high)
+        wide.append(both[:modes] + both[modes:] + dot(four[:modes], block_low))
     for tile in range(tiles):
-        spectra = []
-        for polar in range(polar_count):
-            block = got[pl.ds(polar * azimuth_count, azimuth_count), :, pl.ds(tile * LANES, LANES)]
-            block = block.reshape(azimuth_count * lon_cols, LANES)
-            block_high, block_low = split_bf16(block)
-            both = dot(four, block_high)
-            spectra.append(both[:modes] + both[modes:] + dot(four[:modes], block_low))
-        for quad, spectrum in enumerate(swap(spectra, QUAD_BITS)):
+        spectra = [spectrum[:, tile * LANES : (tile + 1) * LANES] for spectrum in wide]
+        for quad, spectrum in enumerate(swap(spectra, FIELD)):
             rows[pl.ds((tile * polar_count + quad) * modes, modes), :] = spectrum
     count = 2 * tiles * polar_count
     extra = orders - devices
@@ -221,7 +233,7 @@
     dense, tail = count * 3 // 4, count // 4
     used = LANES * 3 // 4
     for row in range(0, count, 8):
-        blocks = swap([coef[order, pl.ds(row, 8), :] for order in range(devices)], LOW_BITS)
+        blocks = swap([coef[order, pl.ds(row, 8), :] for order in range(devices)], 1)
         head = min(max(dense - row, 0), 8)
         for device in range(devices):
             start = device * dense
@@ -236,32 +248,19 @@
                     ]
 
 
-def filter_kernel(first_degree, got, real, imag, sent, real_buf, imag_buf, turned, sems):
-    degrees, channels, _ = real_buf.shape
-    start = first_degree[0]
-    copies = []
-    for degree in range(degrees):
-        pair = [
-            pltpu.make_async_copy(real.at[start + degree], real_buf.at[degree], sems.at[0, degree]),
-            pltpu.make_async_copy(imag.at[start + degree], imag_buf.at[degree], sems.at[1, degree]),
-        ]
-        for copy in pair:
-            copy.start()
-        copies.append(pair)
+def filter_kernel(got, own_filter, sent, turned):
+    _, degrees, channels, _ = own_filter.shape
     tiles = channels // LANES
     count = 8 * tiles
     dense, tail = count * 3 // 4, count // 4
     devices = sent.shape[0] // dense
-    groups = [
-        (tile, top, quad) for tile in range(tiles) for top in range(2) for quad in range(4)
-    ]
-    quarter = lax.broadcasted_iota(jnp.int32, (16, LANES), 1) // 32
+    quarter = lax.broadcasted_iota(jnp.int32, (devices, LANES), 1) // 32
     spectra = []
     for half in range(2):
         parts = []
-        for tile, top, quad in groups:
-            row = 2 * (4 * tile + quad) + half
-            load = lambda start: got[pl.ds(top * 16 * dense + start, 16, stride=dense), :]
+        for own in range(count // 2):
+            row = 2 * own + half
+            load = lambda start: got[pl.ds(start, devices, stride=dense), :]
             if row < dense:
                 parts.append(load(row))
                 continue
@@ -274,15 +273,12 @@
         spectra.append(jnp.concatenate(parts, axis=0).T)
     results = [[None] * 4 for _ in range(2)]
     for degree in range(degrees):
-        for copy in copies[degree]:
-            copy.wait()
         places = [(32 * degree, 32), (64 + 16 * degree, 16)]
         own = jnp.concatenate(
             [spectra[half][start : start + size] for half in range(2) for start, size in places],
             axis=0,
         )
-        by_real = dot3(own, *split_bf16(real_buf[degree]))
-        by_imag = dot3(own, *split_bf16(imag_buf[degree]))
+        by_real, by_imag = (dot3(own, *split_bf16(own_filter[part, degree])) for part in range(2))
         size = 48
         outs = (by_real[:size] - by_imag[size:], by_real[size:] + by_imag[:size])
         for half in range(2):
@@ -292,22 +288,15 @@
     for half in range(2):
         padding = jnp.zeros((32, channels), jnp.float32)
         across.append(jnp.concatenate(results[half] + [padding], axis=0).T)
-    for top in range(2):
-        rows = []
-        for row in range(count):
-            tile, quad, half = row // 8, row // 2 % 4, row % 2
-            start = ((tile * 2 + top) * 4 + quad) * 16
-            rows.append(across[half][start : start + 16])
-        for row in range(dense):
-            part = row // tail
-            folded = pltpu.roll(rows[dense + row % tail], 96 - 32 * part, 1)
-            turned[pl.ds((top * dense + row) * 16, 16), :] = jnp.where(
-                quarter < 3, rows[row], folded
-            )
+    rows = [
+        across[row % 2][row // 2 * devices : (row // 2 + 1) * devices] for row in range(count)
+    ]
+    for row in range(dense):
+        part = row // tail
+        folded = pltpu.roll(rows[dense + row % tail], 96 - 32 * part, 1)
+        turned[pl.ds(row * devices, devices), :] = jnp.where(quarter < 3, rows[row], folded)
     for device in range(devices):
-        sent[pl.ds(device * dense, dense), :] = turned[
-            pl.ds(device // 16 * 16 * dense + device % 16, dense, stride=16), :
-        ]
+        sent[pl.ds(device * dense, dense), :] = turned[pl.ds(device, dense, stride=devices), :]
 
 
 def synthesis_kernel(
@@ -335,10 +324,10 @@
             blocks = [got[pl.ds(device * dense + row, 8), :] for device in range(devices)]
         else:
             blocks = [tails[device] for device in range(devices)]
-        blocks = swap(blocks, LOW_BITS)
+        blocks = swap(blocks, 1)
         for order in range(devices):
             back[order, pl.ds(row, 8), :] = blocks[order]
-    keep = (lax.broadcasted_iota(jnp.int32, (count, LANES), 1) & 64) == 0
+    keep = (lax.broadcasted_iota(jnp.int32, (count, LANES), 1) & 16) == 0
     for order in range(devices):
         both = jnp.concatenate([coef[order], back[order]], axis=0)
         values = dot3(both, leg_high[order], leg_low[order])
@@ -359,7 +348,7 @@
     four = jnp.concatenate([four_high[...], four_low[...]], axis=0)
     points = four_high.shape[0]
     half = points // 2
-    keep = (lax.broadcasted_iota(jnp.int32, (half, LANES), 1) & 64) == 0
+    keep = (lax.broadcasted_iota(jnp.int32, (half, LANES), 1) & 16) == 0
     for tile in range(count // 8):
         states = []
         for quad in range(4):
@@ -371,10 +360,10 @@
             both = dot(four, modes_high)
             values = both[:points] + both[points:] + dot(four[:points], modes_low)
             first, second = values[:half], values[half:]
-            skip = jnp.where(keep, first, pltpu.roll(second, 64, 1))
-            branch = jnp.where(keep, pltpu.roll(first, 64, 1), second)
+            skip = jnp.where(keep, first, pltpu.roll(second, 16, 1))
+            branch = jnp.where(keep, pltpu.roll(first, LANES - 16, 1), second)
             states.append(gelu(branch) + skip)
-        for polar, state in enumerate(swap(states, QUAD_BITS)):
+        for polar, state in enumerate(swap(states, FIELD)):
             for azimuth in range(azimuth_count):
                 device = polar * azimuth_count + azimuth
                 sent[pl.ds(device * dense + tail * tile, tail), :] = state[
@@ -382,11 +371,10 @@
                 ]
 
 
-def mlp_kernel(got, gain, w_in, w_out, mixed, state, result, sem):
-    channels = state.shape[1]
-    _, lat_rows, lon_cols, _ = mixed.shape
+def mlp_kernel(got, gain, w_in, w_out, mixed, state):
+    tiles = state.shape[0]
+    _, lon_cols, lat_rows, _ = mixed.shape
     part = lon_cols // 2
-    tiles = channels // LANES
     devices = got.shape[0] // (tiles * part)
     for tile in range(tiles):
         blocks = swap(
@@ -394,23 +382,25 @@
                 got[pl.ds((device * tiles + tile) * part, part), :]
                 for device in range(devices)
             ],
-            OWNER_BITS,
+            1,
         )
         for device in range(devices):
-            state[pl.ds(part * device, part), pl.ds(tile * LANES, LANES)] = blocks[device]
-    value = state[...]
+            state[tile, pl.ds(part * device, part), :] = blocks[device]
+    value = jnp.concatenate([state[tile] for tile in range(tiles)], axis=1)
     center = jnp.mean(value, axis=-1, keepdims=True)
     spread = jnp.mean((value - center) ** 2, axis=-1, keepdims=True)
-    normed = ((value - center) * lax.rsqrt(spread + 1e-05) * gain[...]).astype(jnp.bfloat16)
+    normed = ((value - center) * lax.rsqrt(spread + 1e-05) * gain[...][None, :]).astype(jnp.bfloat16)
     hidden = gelu(dot(normed, w_in[...])).astype(jnp.bfloat16)
-    state[...] = value + dot(hidden, w_out[...])
+    value = value + dot(hidden, w_out[...])
+    for tile in range(tiles):
+        state[tile] = value[:, tile * LANES : (tile + 1) * LANES]
     for top in range(2):
-        for lat in range(lat_rows):
-            row = part * (top * lat_rows + lat)
-            result[0, lat, pl.ds(top * part, part), :] = state[pl.ds(row, part), :]
-    copy = pltpu.make_async_copy(result, mixed, sem)
-    copy.start()
-    copy.wait()
+        for lon in range(part):
+            for tile in range(tiles):
+                lanes = pl.ds(tile * LANES, LANES)
+                mixed[0, top * part + lon, :, lanes] = state[
+                    tile, pl.ds(top * part * lat_rows + lon, lat_rows, stride=part), :
+                ]
 
 
 def joint_fits(field, filter_real, polar_count, azimuth_count):
@@ -460,8 +450,8 @@
     )
     degree = (degree[None, :] + np.arange(degrees_here)[:, None]).reshape(-1)
     lane = np.arange(LANES)
-    lat_fine = (lane >> 4 & 3) * lat_rows + (lane >> 6) * 16 + (lane & 15)
-    lat_coarse = (lane >> 4 & 3) * lat_out + (lane & 15)
+    lat_fine = lane
+    lat_coarse = lane // 32 * lat_out + lane % 16
     fine = fine[:, degree][:, :, lat_fine].transpose(0, 2, 1)
     coarse = coarse[:, degree][:, :, lat_coarse]
     analyse = np.zeros((devices, 2, LANES, 4, devices))
@@ -492,44 +482,43 @@
     def far(*arrays):
         return [pltpu.with_memory_space_constraint(array, pltpu.HBM) for array in arrays]
 
-    sent = pl.pallas_call(
+    parts = lon_cols // 8 * (channels // LANES)
+    sent, own_filter = pl.pallas_call(
         scatter_kernel,
-        in_specs=[hbm],
-        out_specs=vmem,
-        out_shape=pltpu.VMEM((devices, lon_cols, channels), jnp.float32),
+        in_specs=[hbm] * 3,
+        out_specs=[vmem] * 2,
+        out_shape=[
+            pltpu.VMEM((devices, lon_cols, channels), jnp.float32),
+            pltpu.VMEM((2, degrees_here, channels, channels), jnp.float32),
+        ],
         scratch_shapes=[
-            pltpu.VMEM((lon_cols // 8, lat_rows, 8, channels), jnp.float32),
-            pltpu.SemaphoreType.DMA((lon_cols // 8,)),
+            pltpu.VMEM((parts, lat_rows, 8, LANES), jnp.float32),
+            pltpu.SemaphoreType.DMA((parts,)),
+            pltpu.SemaphoreType.DMA((2,)),
         ],
         compiler_params=pltpu.CompilerParams(vmem_limit_bytes=8 * MIB),
         name="scatter_channels",
-    )(*far(field))
+    )(*far(field, filter_real, filter_imag))
     got = exchange(sent)
     coef, sent = pl.pallas_call(
         functools.partial(analysis_kernel, polar_count),
         in_specs=[vmem] * 5,
-        out_specs=[vmem, vmem],
+        out_specs=[vmem] * 2,
         out_shape=[pltpu.VMEM((devices, count, LANES), jnp.float32), block],
         scratch_shapes=[pltpu.VMEM((count * orders, LANES), jnp.float32)],
         compiler_params=pltpu.CompilerParams(vmem_limit_bytes=8 * MIB),
         name="analysis",
     )(*near(got, *split_constant(forward), *split_constant(analyse)))
     got = exchange(sent)
-    first_degree = (lax.axis_index("polar") * degrees_here).astype(jnp.int32).reshape(1)
     sent = pl.pallas_call(
         filter_kernel,
-        in_specs=[pl.BlockSpec(memory_space=pltpu.SMEM), vmem, hbm, hbm],
+        in_specs=[vmem] * 2,
         out_specs=vmem,
         out_shape=block,
-        scratch_shapes=[
-            pltpu.VMEM((degrees_here, channels, channels), jnp.float32),
-            pltpu.VMEM((degrees_here, channels, channels), jnp.float32),
-            pltpu.VMEM((devices * dense, LANES), jnp.float32),
-            pltpu.SemaphoreType.DMA((2, degrees_here)),
-        ],
+        scratch_shapes=[pltpu.VMEM((devices * dense, LANES), jnp.float32)],
         compiler_params=pltpu.CompilerParams(vmem_limit_bytes=8 * MIB),
         name="channel_filter",
-    )(first_degree, *near(got), *far(filter_real, filter_imag))
+    )(*near(got, own_filter))
     got = exchange(sent)
     sent = pl.pallas_call(
         functools.partial(synthesis_kernel, polar_count),
@@ -545,20 +534,16 @@
         name="synthesis",
     )(*near(got, coef, *split_constant(backward), *split_constant(synthesise)))
     got = exchange(sent)
-    result = (1, lat_out, lon_out, channels)
-    return pl.pallas_call(
+    mixed = pl.pallas_call(
         mlp_kernel,
         in_specs=[vmem] * 4,
-        out_specs=pl.BlockSpec(memory_space=pl.ANY),
-        out_shape=jax.ShapeDtypeStruct(result, jnp.float32),
-        scratch_shapes=[
-            pltpu.VMEM((lat_out * lon_out, channels), jnp.float32),
-            pltpu.VMEM(result, jnp.float32),
-            pltpu.SemaphoreType.DMA,
-        ],
+        out_specs=vmem,
+        out_shape=jax.ShapeDtypeStruct((1, lon_out, lat_out, channels), jnp.float32),
+        scratch_shapes=[pltpu.VMEM((channels // LANES, lat_out * lon_out, LANES), jnp.float32)],
         compiler_params=pltpu.CompilerParams(vmem_limit_bytes=8 * MIB),
         name="mlp",
-    )(*near(got, norm_gain.reshape(1, channels), w_in, w_out))
+    )(*near(got, norm_gain, w_in, w_out))
+    return mixed.transpose(0, 2, 1, 3)
 
 
 def per_device(field, filter_real, filter_imag, norm_gain, w_in, w_out):

time: 94.3 us -> 88.2 us (0.935)
  blocking collectives: 50.9 us -> 78 us
  waiting for transfers between devices: 22.8 us -> 0 us
  starting transfers between devices: 5.18 us -> 0 us
  Pallas kernels: 14 us -> 9.77 us
    all_to_all x2 -> x4, blocking collectives: 50.9 us -> 78 us  [exchange(): moved = lax.all_to_all(split, BOTH, split_axis=0, concat_axis=0, tiled=True)]
    all_to_all x2 -> x0, waiting for transfers between devices: 22.8 us -> none  [exchange(): moved = lax.all_to_all(split, BOTH, split_axis=0, concat_axis=0, tiled=True)]
    all_to_all x2 -> x0, starting transfers between devices: 5.18 us -> none  [exchange(): moved = lax.all_to_all(split, BOTH, split_axis=0, concat_axis=0, tiled=True)]
    pallas_call x3, Pallas kernels: 8.19 us -> 6.13 us  [the longest x1 2.98 us: jointly(): pl.pallas_call(scatter_kernel, in_specs=[hbm] * 3, out_specs=[vmem] * 2,...]
    pallas_call x1, Pallas kernels: 2.95 us -> 1.84 us  [jointly(): pl.pallas_call(functools.partial(synthesis_kernel, polar_count), in_specs...]
    pallas_call x1, Pallas kernels: 2.89 us -> 1.8 us  [jointly(): pl.pallas_call(functools.partial(analysis_kernel, polar_count), in_specs=...]
  transfers between devices with their start and end apart: 2 -> 0, of which waited for: 2 -> 0; matrix products, arithmetic and copies ran while one was open for 0% -> 0% of each run, Pallas kernels for 0% -> 0%
where the time goes in v2:
time: 88.2 us; the launch traced here: 88 us
  blocking collectives  78 us (88%)
  Pallas kernels  9.77 us (11%)
    all_to_all x4, blocking collectives, exchange(): moved = lax.all_to_all(split, BOTH, split_axis=0, concat_axis=0, tiled=True)  78 us
    pallas_call x1, Pallas kernels, jointly(): pl.pallas_call(scatter_kernel, in_specs=[hbm] * 3, out_specs=[vmem] * 2,...  2.98 us
    pallas_call x1, Pallas kernels, jointly(): pl.pallas_call(functools.partial(synthesis_kernel, polar_count), in_specs...  1.84 us
    pallas_call x1, Pallas kernels, jointly(): pl.pallas_call(mlp_kernel, in_specs=[vmem] * 4, out_specs=vmem, out_shape...  1.81 us
    pallas_call x1, Pallas kernels, jointly(): pl.pallas_call(functools.partial(analysis_kernel, polar_count), in_specs=...  1.8 us

profile of v2, /device:TPU:0, one launch (start us, length us, event | category | flops | bytes accessed | tf_op | source)
XLA Modules:
  0.0 88.0 jit_solution(12833387693398590481)
XLA Ops:
  0.0 0.0 copy-start.3
  0.0 3.0 %scatter_channels.1 = (f32[32,24,384]{2,1,0:T(8,128)S(1)}, f32[2,2,384,384]{3,2,1,0:T(8,128)S(1)}) custom-call(f32[1,32,24,384]{3,2,1,0:T(8,128)} %field.1, f32[8,384,384]{2,1,0:T(8,128)} %real.1, f32[8,384,384]{2,1,0:T(8,128)} %imag.1), custom_call_target="tpu_custom_call" | custom-call | tf_op jit(solution)/shard_map/scatter_channels/pallas_call | solution.py:486
  3.0 0.0 copy-start.2
  3.0 0.0 copy-start.6
  3.0 0.0 copy-start.7
  3.0 37.5 %all_to_all.20.got = f32[32,24,384]{2,1,0:T(8,128)S(1)} all-to-all(f32[32,24,384]{2,1,0:T(8,128)S(1)} %get-tuple-element.9), channel_id=1, replica_groups=mesh['polar'=4,'azimuth'=8] {'polar','azimuth'}, dimensions={0} | all-to-all | bytes 2359296 | tf_op jit(solution)/shard_map/all_to_all | solution.py:476
  40.5 0.0 copy-done.3
  40.5 0.0 copy-done.2
  40.5 0.0 copy-done.6
  40.5 0.0 copy-done.7
  40.5 0.0 copy-start.1
  40.6 1.8 %analysis.1 = (f32[32,24,128]{2,1,0:T(8,128)S(1)}, f32[576,128]{1,0:T(8,128)S(1)}) custom-call(f32[32,24,384]{2,1,0:T(8,128)S(1)} %all_to_all.20.got, bf16[96,192]{1,0:T(8,128)(2,1)S(1)} %copy-done.7, bf16[96,192]{1,0:T(8,128)(2,1)S(1)} %copy-done.6, bf16[32,256,128]{2,1,0:T(8,128)(2,1)S(1)} %copy-done.3, bf16[32,256,128]{2,1,0:T(8,128)(2,1)S(1)} %copy-done.2), custom_call_target="tpu_custom_call" | custom-call | tf_op jit(solution)/shard_map/analysis/pallas_call | solution.py:503
  42.4 0.0 copy-start
  42.4 0.0 copy-start.8
  42.4 0.0 copy-start.9
  42.4 13.5 %all_to_all.21 = f32[32,9,2,128]{3,2,1,0:T(2,128)S(1)} all-to-all(f32[32,9,2,128]{3,2,1,0:T(2,128)S(1)} %bitcast.12), channel_id=1, replica_groups=mesh['polar'=4,'azimuth'=8] {'polar','azimuth'}, dimensions={0} | all-to-all | bytes 589824 | tf_op jit(solution)/shard_map/all_to_all | solution.py:476
  55.9 1.3 %channel_filter.1 = f32[576,128]{1,0:T(8,128)S(1)} custom-call(f32[576,128]{1,0:T(8,128)S(1)} %bitcast.9, f32[2,2,384,384]{3,2,1,0:T(8,128)S(1)} %get-tuple-element.11.own_filter), custom_call_target="tpu_custom_call" | custom-call | tf_op jit(solution)/shard_map/channel_filter/pallas_call | solution.py:513
  57.3 13.5 %all_to_all.22 = f32[32,9,2,128]{3,2,1,0:T(2,128)S(1)} all-to-all(f32[32,9,2,128]{3,2,1,0:T(2,128)S(1)} %bitcast.10), channel_id=1, replica_groups=mesh['polar'=4,'azimuth'=8] {'polar','azimuth'}, dimensions={0} | all-to-all | bytes 589824 | tf_op jit(solution)/shard_map/all_to_all | solution.py:476
  70.8 0.0 copy-done.1
  70.8 0.0 copy-done
  70.8 0.0 copy-done.8
  70.8 0.0 copy-done.9
  70.8 0.0 copy-start.4
  70.8 0.0 copy-start.5
  70.8 0.0 copy-start.10
  70.8 1.8 %synthesis.1 = f32[576,128]{1,0:T(8,128)S(1)} custom-call(f32[576,128]{1,0:T(8,128)S(1)} %bitcast.7, f32[32,24,128]{2,1,0:T(8,128)S(1)} %get-tuple-element.12.coef, bf16[96,96]{1,0:T(8,128)(2,1)S(1)} %copy-done.9, bf16[96,96]{1,0:T(8,128)(2,1)S(1)} %copy-done.8, bf16[32,128,256]{2,1,0:T(8,128)(2,1)S(1)} %copy-done.1, bf16[32,128,256]{2,1,0:T(8,128)(2,1)S(1)} %copy-done), custom_call_target="tpu_custom_call" | custom-call | tf_op jit(solution)/shard_map/synthesis/pallas_call | solution.py:523
  72.7 13.5 %all_to_all.23 = f32[32,9,2,128]{3,2,1,0:T(2,128)S(1)} all-to-all(f32[32,9,2,128]{3,2,1,0:T(2,128)S(1)} %bitcast.8), channel_id=1, replica_groups=mesh['polar'=4,'azimuth'=8] {'polar','azimuth'}, dimensions={0} | all-to-all | bytes 589824 | tf_op jit(solution)/shard_map/all_to_all | solution.py:476
  86.2 0.0 copy-done.4
  86.2 0.0 copy-done.5
  86.2 0.0 copy-done.10
  86.2 1.8 %mlp.1 = f32[1,12,16,384]{3,2,1,0:T(8,128)} custom-call(f32[576,128]{1,0:T(8,128)S(1)} %bitcast.11, f32[384]{0:T(512)S(1)} %copy-done.10, bf16[384,768]{1,0:T(8,128)(2,1)S(1)} %copy-done.4, bf16[768,384]{1,0:T(8,128)(2,1)S(1)} %copy-done.5), custom_call_target="tpu_custom_call" | custom-call | tf_op jit(solution)/shard_map/mlp/pallas_call | solution.py:537
Async XLA Ops:
  0.0 40.5 %copy-start.3 = (bf16[32,256,128]{2,1,0:T(8,128)(2,1)S(1)}, bf16[32,256,128]{2,1,0:T(8,128)(2,1)}, u32[]{:S(2)}) copy-start(bf16[32,256,128]{2,1,0:T(8,128)(2,1)} %constant.18.clone.leg_high) | copy-start | bytes 6291460
  3.0 37.5 %copy-start.2 = (bf16[32,256,128]{2,1,0:T(8,128)(2,1)S(1)}, bf16[32,256,128]{2,1,0:T(8,128)(2,1)}, u32[]{:S(2)}) copy-start(bf16[32,256,128]{2,1,0:T(8,128)(2,1)} %constant.19.clone.leg_low) | copy-start | bytes 6291460
  3.0 37.5 %copy-start.6 = (bf16[96,192]{1,0:T(8,128)(2,1)S(1)}, bf16[96,192]{1,0:T(8,128)(2,1)}, u32[]{:S(2)}) copy-start(bf16[96,192]{1,0:T(8,128)(2,1)} %constant.17.clone.four_low) | copy-start | bytes 110596
  3.0 37.5 %copy-start.7 = (bf16[96,192]{1,0:T(8,128)(2,1)S(1)}, bf16[96,192]{1,0:T(8,128)(2,1)}, u32[]{:S(2)}) copy-start(bf16[96,192]{1,0:T(8,128)(2,1)} %constant.16.clone.four_high) | copy-start | bytes 110596
  40.5 30.2 %copy-start.1 = (bf16[32,128,256]{2,1,0:T(8,128)(2,1)S(1)}, bf16[32,128,256]{2,1,0:T(8,128)(2,1)}, u32[]{:S(2)}) copy-start(bf16[32,128,256]{2,1,0:T(8,128)(2,1)} %constant.22.clone.leg_high) | copy-start | bytes 6291460
  42.4 28.4 %copy-start = (bf16[32,128,256]{2,1,0:T(8,128)(2,1)S(1)}, bf16[32,128,256]{2,1,0:T(8,128)(2,1)}, u32[]{:S(2)}) copy-start(bf16[32,128,256]{2,1,0:T(8,128)(2,1)} %constant.23.clone.leg_low) | copy-start | bytes 6291460
  42.4 28.4 %copy-start.8 = (bf16[96,96]{1,0:T(8,128)(2,1)S(1)}, bf16[96,96]{1,0:T(8,128)(2,1)}, u32[]{:S(2)}) copy-start(bf16[96,96]{1,0:T(8,128)(2,1)} %constant.21.clone.four_low) | copy-start | bytes 55300
  42.4 28.4 %copy-start.9 = (bf16[96,96]{1,0:T(8,128)(2,1)S(1)}, bf16[96,96]{1,0:T(8,128)(2,1)}, u32[]{:S(2)}) copy-start(bf16[96,96]{1,0:T(8,128)(2,1)} %constant.20.clone.four_high) | copy-start | bytes 55300
  70.8 15.4 %copy-start.4 = (bf16[384,768]{1,0:T(8,128)(2,1)S(1)}, bf16[384,768]{1,0:T(8,128)(2,1)}, u32[]{:S(2)}) copy-start(bf16[384,768]{1,0:T(8,128)(2,1)} %w_in.1) | copy-start | bytes 1769476
  70.8 15.4 %copy-start.5 = (bf16[768,384]{1,0:T(8,128)(2,1)S(1)}, bf16[768,384]{1,0:T(8,128)(2,1)}, u32[]{:S(2)}) copy-start(bf16[768,384]{1,0:T(8,128)(2,1)} %w_out.1) | copy-start | bytes 1769476
  70.8 15.4 %copy-start.10 = (f32[384]{0:T(512)S(1)}, f32[384]{0:T(512)}, u32[]{:S(2)}) copy-start(f32[384]{0:T(512)} %gain.1) | copy-start | bytes 4612

commit v3 on v2

--- a/solution.py
+++ b/solution.py
@@ -221,10 +221,20 @@
             rows[pl.ds((tile * polar_count + quad) * modes, modes), :] = spectrum
     count = 2 * tiles * polar_count
     extra = orders - devices
-    for order in range(devices):
-        first = rows[pl.ds(order, count, stride=orders), :]
-        second = rows[pl.ds(devices + order % extra, count, stride=orders), :]
-        coef[order] = dot3(jnp.concatenate([first, second], axis=1), leg_high[order], leg_low[order])
+    first_half = lax.broadcasted_iota(jnp.int32, (count, LANES), 1) < LANES // 2
+    for order in range(extra):
+        own = [
+            rows[pl.ds(row, count, stride=orders), :]
+            for row in (order, order + extra, devices + order)
+        ]
+        values = dot3(jnp.concatenate(own, axis=0), leg_high[order], leg_low[order])
+        for part in range(2):
+            lanes = slice(part * LANES, (part + 1) * LANES)
+            coef[order + part * extra] = jnp.where(
+                first_half,
+                values[part * count : (part + 1) * count, lanes],
+                values[2 * count :, lanes],
+            )
     pack_by_degree(coef, sent)
 
 
@@ -278,7 +288,9 @@
             [spectra[half][start : start + size] for half in range(2) for start, size in places],
             axis=0,
         )
-        by_real, by_imag = (dot3(own, *split_bf16(own_filter[part, degree])) for part in range(2))
+        parts = [split_bf16(own_filter[part, degree]) for part in range(2)]
+        both = dot3(own, *(jnp.concatenate(pair, axis=1) for pair in zip(*parts)))
+        by_real, by_imag = both[:, :channels], both[:, channels:]
         size = 48
         outs = (by_real[:size] - by_imag[size:], by_real[size:] + by_imag[:size])
         for half in range(2):
@@ -371,7 +383,7 @@
                 ]
 
 
-def mlp_kernel(got, gain, w_in, w_out, mixed, state):
+def mlp_kernel(got, gain, w_in, w_out, mixed, state, result, sems):
     tiles = state.shape[0]
     _, lon_cols, lat_rows, _ = mixed.shape
     part = lon_cols // 2
@@ -386,21 +398,26 @@
         )
         for device in range(devices):
             state[tile, pl.ds(part * device, part), :] = blocks[device]
-    value = jnp.concatenate([state[tile] for tile in range(tiles)], axis=1)
-    center = jnp.mean(value, axis=-1, keepdims=True)
-    spread = jnp.mean((value - center) ** 2, axis=-1, keepdims=True)
-    normed = ((value - center) * lax.rsqrt(spread + 1e-05) * gain[...][None, :]).astype(jnp.bfloat16)
-    hidden = gelu(dot(normed, w_in[...])).astype(jnp.bfloat16)
-    value = value + dot(hidden, w_out[...])
-    for tile in range(tiles):
-        state[tile] = value[:, tile * LANES : (tile + 1) * LANES]
+    copies = []
     for top in range(2):
-        for lon in range(part):
-            for tile in range(tiles):
-                lanes = pl.ds(tile * LANES, LANES)
-                mixed[0, top * part + lon, :, lanes] = state[
+        cells = pl.ds(top * part * lat_rows, part * lat_rows)
+        value = jnp.concatenate([state[tile, cells, :] for tile in range(tiles)], axis=1)
+        center = jnp.mean(value, axis=-1, keepdims=True)
+        spread = jnp.mean((value - center) ** 2, axis=-1, keepdims=True)
+        normed = (value - center) * lax.rsqrt(spread + 1e-05) * gain[...][None, :]
+        hidden = gelu(dot(normed.astype(jnp.bfloat16), w_in[...])).astype(jnp.bfloat16)
+        value = value + dot(hidden, w_out[...])
+        for tile in range(tiles):
+            state[tile, cells, :] = value[:, tile * LANES : (tile + 1) * LANES]
+            for lon in range(part):
+                result[top * part + lon, :, pl.ds(tile * LANES, LANES)] = state[
                     tile, pl.ds(top * part * lat_rows + lon, lat_rows, stride=part), :
                 ]
+        lons = pl.ds(top * part, part)
+        copies.append(pltpu.make_async_copy(result.at[lons], mixed.at[0, lons], sems.at[top]))
+        copies[-1].start()
+    for copy in copies:
+        copy.wait()
 
 
 def joint_fits(field, filter_real, polar_count, azimuth_count):
@@ -454,16 +471,16 @@
     lat_coarse = lane // 32 * lat_out + lane % 16
     fine = fine[:, degree][:, :, lat_fine].transpose(0, 2, 1)
     coarse = coarse[:, degree][:, :, lat_coarse]
-    analyse = np.zeros((devices, 2, LANES, 4, devices))
+    analyse = np.zeros((extra, LANES, 2, 4, devices))
     synthesise = np.zeros((devices, 4, devices, 2, LANES))
     for order in range(devices):
         later, which = devices + order % extra, order // extra
         own = slice(which * devices, (which + 1) * devices)
-        analyse[order, 0, :, :2] = fine[order].reshape(LANES, 2, devices)
-        analyse[order, 1, :, 2] = fine[later][:, own]
+        analyse[order % extra, :, which, :2] = fine[order].reshape(LANES, 2, devices)
+        analyse[order % extra, :, which, 2] = fine[later][:, own]
         synthesise[order, :2, :, 0] = coarse[order].reshape(2, devices, LANES)
         synthesise[order, 2, :, 1] = coarse[later][own]
-    analyse = analyse.reshape(devices, 2 * LANES, LANES)
+    analyse = analyse.reshape(extra, LANES, 2 * LANES)
     synthesise = synthesise.reshape(devices, LANES, 2 * LANES)
 
     vmem = pl.BlockSpec(memory_space=pltpu.VMEM)
@@ -537,9 +554,13 @@
     mixed = pl.pallas_call(
         mlp_kernel,
         in_specs=[vmem] * 4,
-        out_specs=vmem,
+        out_specs=pl.BlockSpec(memory_space=pl.ANY),
         out_shape=jax.ShapeDtypeStruct((1, lon_out, lat_out, channels), jnp.float32),
-        scratch_shapes=[pltpu.VMEM((channels // LANES, lat_out * lon_out, LANES), jnp.float32)],
+        scratch_shapes=[
+            pltpu.VMEM((channels // LANES, lat_out * lon_out, LANES), jnp.float32),
+            pltpu.VMEM((lon_out, lat_out, channels), jnp.float32),
+            pltpu.SemaphoreType.DMA((2,)),
+        ],
         compiler_params=pltpu.CompilerParams(vmem_limit_bytes=8 * MIB),
         name="mlp",
     )(*near(got, norm_gain, w_in, w_out))

time: 88.2 us -> 87.9 us (level)
  no operation moved by 1% of the time
where the time goes in v3:
time: 87.9 us; the launch traced here: 87.7 us
  blocking collectives  78 us (89%)
  Pallas kernels  9.4 us (11%)
    all_to_all x4, blocking collectives, exchange(): moved = lax.all_to_all(split, BOTH, split_axis=0, concat_axis=0, tiled=True)  78 us
    pallas_call x1, Pallas kernels, jointly(): pl.pallas_call(scatter_kernel, in_specs=[hbm] * 3, out_specs=[vmem] * 2,...  2.83 us
    pallas_call x1, Pallas kernels, jointly(): pl.pallas_call(mlp_kernel, in_specs=[vmem] * 4, out_specs=pl.BlockSpec(me...  1.85 us
    pallas_call x1, Pallas kernels, jointly(): pl.pallas_call(functools.partial(synthesis_kernel, polar_count), in_specs...  1.83 us

profile of v3, /device:TPU:0, one launch (start us, length us, event | category | flops | bytes accessed | tf_op | source)
XLA Modules:
  0.0 87.7 jit_solution(1759371503395625083)
XLA Ops:
  0.0 2.8 %scatter_channels.1 = (f32[32,24,384]{2,1,0:T(8,128)S(1)}, f32[2,2,384,384]{3,2,1,0:T(8,128)S(1)}) custom-call(f32[1,32,24,384]{3,2,1,0:T(8,128)} %field.1, f32[8,384,384]{2,1,0:T(8,128)} %real.1, f32[8,384,384]{2,1,0:T(8,128)} %imag.1), custom_call_target="tpu_custom_call" | custom-call | tf_op jit(solution)/shard_map/scatter_channels/pallas_call | solution.py:503
  2.8 0.0 copy-start.2
  2.8 0.0 copy-start.3
  2.9 0.0 copy-start.6
  2.9 0.0 copy-start.7
  2.9 37.5 %all_to_all.20.got = f32[32,24,384]{2,1,0:T(8,128)S(1)} all-to-all(f32[32,24,384]{2,1,0:T(8,128)S(1)} %get-tuple-element.9), channel_id=1, replica_groups=mesh['polar'=4,'azimuth'=8] {'polar','azimuth'}, dimensions={0} | all-to-all | bytes 2359296 | tf_op jit(solution)/shard_map/all_to_all | solution.py:493
  40.4 0.0 copy-done.2
  40.4 0.0 copy-done.3
  40.4 0.0 copy-done.6
  40.4 0.0 copy-done.7
  40.4 0.0 copy-start.1
  40.4 1.6 %analysis.1 = (f32[32,24,128]{2,1,0:T(8,128)S(1)}, f32[576,128]{1,0:T(8,128)S(1)}) custom-call(f32[32,24,384]{2,1,0:T(8,128)S(1)} %all_to_all.20.got, bf16[96,192]{1,0:T(8,128)(2,1)S(1)} %copy-done.7, bf16[96,192]{1,0:T(8,128)(2,1)S(1)} %copy-done.6, bf16[16,128,256]{2,1,0:T(8,128)(2,1)S(1)} %copy-done.3, bf16[16,128,256]{2,1,0:T(8,128)(2,1)S(1)} %copy-done.2), custom_call_target="tpu_custom_call" | custom-call | tf_op jit(solution)/shard_map/analysis/pallas_call | solution.py:520
  42.1 0.0 copy-start
  42.1 0.0 copy-start.8
  42.1 0.0 copy-start.9
  42.1 13.5 %all_to_all.21 = f32[32,9,2,128]{3,2,1,0:T(2,128)S(1)} all-to-all(f32[32,9,2,128]{3,2,1,0:T(2,128)S(1)} %bitcast.12), channel_id=1, replica_groups=mesh['polar'=4,'azimuth'=8] {'polar','azimuth'}, dimensions={0} | all-to-all | bytes 589824 | tf_op jit(solution)/shard_map/all_to_all | solution.py:493
  55.6 1.3 %channel_filter.1 = f32[576,128]{1,0:T(8,128)S(1)} custom-call(f32[576,128]{1,0:T(8,128)S(1)} %bitcast.9, f32[2,2,384,384]{3,2,1,0:T(8,128)S(1)} %get-tuple-element.11.own_filter), custom_call_target="tpu_custom_call" | custom-call | tf_op jit(solution)/shard_map/channel_filter/pallas_call | solution.py:530
  56.9 13.5 %all_to_all.22 = f32[32,9,2,128]{3,2,1,0:T(2,128)S(1)} all-to-all(f32[32,9,2,128]{3,2,1,0:T(2,128)S(1)} %bitcast.10), channel_id=1, replica_groups=mesh['polar'=4,'azimuth'=8] {'polar','azimuth'}, dimensions={0} | all-to-all | bytes 589824 | tf_op jit(solution)/shard_map/all_to_all | solution.py:493
  70.4 0.0 copy-done.1
  70.4 0.0 copy-done
  70.4 0.0 copy-done.8
  70.4 0.0 copy-done.9
  70.4 0.0 copy-start.4
  70.4 0.0 copy-start.5
  70.4 0.0 copy-start.10
  70.4 1.8 %synthesis.1 = f32[576,128]{1,0:T(8,128)S(1)} custom-call(f32[576,128]{1,0:T(8,128)S(1)} %bitcast.7, f32[32,24,128]{2,1,0:T(8,128)S(1)} %get-tuple-element.12.coef, bf16[96,96]{1,0:T(8,128)(2,1)S(1)} %copy-done.9, bf16[96,96]{1,0:T(8,128)(2,1)S(1)} %copy-done.8, bf16[32,128,256]{2,1,0:T(8,128)(2,1)S(1)} %copy-done.1, bf16[32,128,256]{2,1,0:T(8,128)(2,1)S(1)} %copy-done), custom_call_target="tpu_custom_call" | custom-call | tf_op jit(solution)/shard_map/synthesis/pallas_call | solution.py:540
  72.3 13.5 %all_to_all.23 = f32[32,9,2,128]{3,2,1,0:T(2,128)S(1)} all-to-all(f32[32,9,2,128]{3,2,1,0:T(2,128)S(1)} %bitcast.8), channel_id=1, replica_groups=mesh['polar'=4,'azimuth'=8] {'polar','azimuth'}, dimensions={0} | all-to-all | bytes 589824 | tf_op jit(solution)/shard_map/all_to_all | solution.py:493
  85.8 0.0 copy-done.4
  85.8 0.0 copy-done.5
  85.8 0.0 copy-done.10
  85.8 1.9 %mlp.1 = f32[1,12,16,384]{3,2,1,0:T(8,128)} custom-call(f32[576,128]{1,0:T(8,128)S(1)} %bitcast.11, f32[384]{0:T(512)S(1)} %copy-done.10, bf16[384,768]{1,0:T(8,128)(2,1)S(1)} %copy-done.4, bf16[768,384]{1,0:T(8,128)(2,1)S(1)} %copy-done.5), custom_call_target="tpu_custom_call" | custom-call | tf_op jit(solution)/shard_map/mlp/pallas_call | solution.py:554
Async XLA Ops:
  2.8 37.6 %copy-start.2 = (bf16[16,128,256]{2,1,0:T(8,128)(2,1)S(1)}, bf16[16,128,256]{2,1,0:T(8,128)(2,1)}, u32[]{:S(2)}) copy-start(bf16[16,128,256]{2,1,0:T(8,128)(2,1)} %constant.19.clone.leg_low) | copy-start | bytes 3145732
  2.8 37.5 %copy-start.3 = (bf16[16,128,256]{2,1,0:T(8,128)(2,1)S(1)}, bf16[16,128,256]{2,1,0:T(8,128)(2,1)}, u32[]{:S(2)}) copy-start(bf16[16,128,256]{2,1,0:T(8,128)(2,1)} %constant.18.clone.leg_high) | copy-start | bytes 3145732
  2.9 37.5 %copy-start.6 = (bf16[96,192]{1,0:T(8,128)(2,1)S(1)}, bf16[96,192]{1,0:T(8,128)(2,1)}, u32[]{:S(2)}) copy-start(bf16[96,192]{1,0:T(8,128)(2,1)} %constant.17.clone.four_low) | copy-start | bytes 110596
  2.9 37.5 %copy-start.7 = (bf16[96,192]{1,0:T(8,128)(2,1)S(1)}, bf16[96,192]{1,0:T(8,128)(2,1)}, u32[]{:S(2)}) copy-start(bf16[96,192]{1,0:T(8,128)(2,1)} %constant.16.clone.four_high) | copy-start | bytes 110596
  40.4 30.0 %copy-start.1 = (bf16[32,128,256]{2,1,0:T(8,128)(2,1)S(1)}, bf16[32,128,256]{2,1,0:T(8,128)(2,1)}, u32[]{:S(2)}) copy-start(bf16[32,128,256]{2,1,0:T(8,128)(2,1)} %constant.22.clone.leg_high) | copy-start | bytes 6291460
  42.1 28.3 %copy-start = (bf16[32,128,256]{2,1,0:T(8,128)(2,1)S(1)}, bf16[32,128,256]{2,1,0:T(8,128)(2,1)}, u32[]{:S(2)}) copy-start(bf16[32,128,256]{2,1,0:T(8,128)(2,1)} %constant.23.clone.leg_low) | copy-start | bytes 6291460
  42.1 28.3 %copy-start.8 = (bf16[96,96]{1,0:T(8,128)(2,1)S(1)}, bf16[96,96]{1,0:T(8,128)(2,1)}, u32[]{:S(2)}) copy-start(bf16[96,96]{1,0:T(8,128)(2,1)} %constant.21.clone.four_low) | copy-start | bytes 55300
  42.1 28.3 %copy-start.9 = (bf16[96,96]{1,0:T(8,128)(2,1)S(1)}, bf16[96,96]{1,0:T(8,128)(2,1)}, u32[]{:S(2)}) copy-start(bf16[96,96]{1,0:T(8,128)(2,1)} %constant.20.clone.four_high) | copy-start | bytes 55300
  70.4 15.4 %copy-start.4 = (bf16[384,768]{1,0:T(8,128)(2,1)S(1)}, bf16[384,768]{1,0:T(8,128)(2,1)}, u32[]{:S(2)}) copy-start(bf16[384,768]{1,0:T(8,128)(2,1)} %w_in.1) | copy-start | bytes 1769476
  70.4 15.4 %copy-start.5 = (bf16[768,384]{1,0:T(8,128)(2,1)S(1)}, bf16[768,384]{1,0:T(8,128)(2,1)}, u32[]{:S(2)}) copy-start(bf16[768,384]{1,0:T(8,128)(2,1)} %w_out.1) | copy-start | bytes 1769476
  70.4 15.4 %copy-start.10 = (f32[384]{0:T(512)S(1)}, f32[384]{0:T(512)}, u32[]{:S(2)}) copy-start(f32[384]{0:T(512)} %gain.1) | copy-start | bytes 4612

commit v4 on v3

--- a/solution.py
+++ b/solution.py
@@ -143,14 +143,16 @@
     return both[:rows] + both[rows:] + dot(left_high, right_low)
 
 
-def swap(blocks, step):
+def swap(blocks, step, before=0, after=0, begin=True, finish=True):
     count = len(blocks)
     axis = len(blocks[0].shape) - 1
-    turn = lambda block, fields: (
-        pltpu.roll(block, fields * step % LANES, axis) if fields * step % LANES else block
-    )
+
+    def turn(block, fields, lanes, wanted):
+        amount = (fields * step * wanted + lanes) % LANES
+        return block if isinstance(amount, int) and amount == 0 else pltpu.roll(block, amount, axis)
+
     place = lax.broadcasted_iota(jnp.int32, blocks[0].shape, axis) // step
-    turned = [turn(blocks[-index % count], -index % count) for index in range(count)]
+    turned = [turn(blocks[-index % count], -index % count, before, begin) for index in range(count)]
     shift = 1
     while shift < count:
         take = (place & shift) != 0
@@ -158,7 +160,11 @@
             jnp.where(take, turned[(index - shift) % count], turned[index]) for index in range(count)
         ]
         shift *= 2
-    return [turn(block, -index) for index, block in enumerate(turned)]
+    return [turn(block, -index, after, finish) for index, block in enumerate(turned)]
+
+
+def own_index(azimuth_count):
+    return lax.axis_index("polar") * azimuth_count + lax.axis_index("azimuth")
 
 
 QUAD = 4
@@ -171,13 +177,10 @@
 
 def scatter_kernel(field, real, imag, sent, own_filter, buf, sems, filter_sems):
     devices, rows, channels = sent.shape
-    parts = [(row, tile) for row in range(rows // 8) for tile in range(channels // LANES)]
     copies = []
-    for index, (row, tile) in enumerate(parts):
+    for row in range(rows // 8):
         copy = pltpu.make_async_copy(
-            field.at[0, :, pl.ds(8 * row, 8), pl.ds(tile * LANES, LANES)],
-            buf.at[index],
-            sems.at[index],
+            field.at[0, :, pl.ds(8 * row, 8), :], buf.at[row], sems.at[row]
         )
         copy.start()
         copies.append(copy)
@@ -191,11 +194,13 @@
     ]
     for copy in filter_copies:
         copy.start()
-    for index, (row, tile) in enumerate(parts):
-        copies[index].wait()
-        blocks = swap([buf[index, lat] for lat in range(devices)], 1)
-        for device in range(devices):
-            sent[device, pl.ds(8 * row, 8), pl.ds(tile * LANES, LANES)] = blocks[device]
+    for row, copy in enumerate(copies):
+        copy.wait()
+        for tile in range(channels // LANES):
+            lanes = pl.ds(tile * LANES, LANES)
+            blocks = swap([buf[row, lat, :, lanes] for lat in range(devices)], 1, finish=False)
+            for device in range(devices):
+                sent[device, pl.ds(8 * row, 8), lanes] = blocks[device]
     for copy in filter_copies:
         copy.wait()
 
@@ -209,6 +214,7 @@
     orders = modes // 2
     four = jnp.concatenate([four_high[...], four_low[...]], axis=0)
     tiles = width // LANES
+    own_turn = LANES - own_index(azimuth_count)
     wide = []
     for polar in range(polar_count):
         block = got[pl.ds(polar * azimuth_count, azimuth_count)]
@@ -217,11 +223,11 @@
         wide.append(both[:modes] + both[modes:] + dot(four[:modes], block_low))
     for tile in range(tiles):
         spectra = [spectrum[:, tile * LANES : (tile + 1) * LANES] for spectrum in wide]
-        for quad, spectrum in enumerate(swap(spectra, FIELD)):
+        for quad, spectrum in enumerate(swap(spectra, FIELD, before=own_turn)):
             rows[pl.ds((tile * polar_count + quad) * modes, modes), :] = spectrum
     count = 2 * tiles * polar_count
     extra = orders - devices
-    first_half = lax.broadcasted_iota(jnp.int32, (count, LANES), 1) < LANES // 2
+    lane = lax.broadcasted_iota(jnp.int32, (count, LANES), 1)
     for order in range(extra):
         own = [
             rows[pl.ds(row, count, stride=orders), :]
@@ -230,8 +236,9 @@
         values = dot3(jnp.concatenate(own, axis=0), leg_high[order], leg_low[order])
         for part in range(2):
             lanes = slice(part * LANES, (part + 1) * LANES)
-            coef[order + part * extra] = jnp.where(
-                first_half,
+            index = order + part * extra
+            coef[index] = jnp.where(
+                ((lane - index) & (LANES - 1)) < LANES // 2,
                 values[part * count : (part + 1) * count, lanes],
                 values[2 * count :, lanes],
             )
@@ -243,7 +250,7 @@
     dense, tail = count * 3 // 4, count // 4
     used = LANES * 3 // 4
     for row in range(0, count, 8):
-        blocks = swap([coef[order, pl.ds(row, 8), :] for order in range(devices)], 1)
+        blocks = swap([coef[order, pl.ds(row, 8), :] for order in range(devices)], 1, begin=False)
         head = min(max(dense - row, 0), 8)
         for device in range(devices):
             start = device * dense
@@ -336,7 +343,7 @@
             blocks = [got[pl.ds(device * dense + row, 8), :] for device in range(devices)]
         else:
             blocks = [tails[device] for device in range(devices)]
-        blocks = swap(blocks, 1)
+        blocks = swap(blocks, 1, finish=False)
         for order in range(devices):
             back[order, pl.ds(row, 8), :] = blocks[order]
     keep = (lax.broadcasted_iota(jnp.int32, (count, LANES), 1) & 16) == 0
@@ -375,7 +382,7 @@
             skip = jnp.where(keep, first, pltpu.roll(second, 16, 1))
             branch = jnp.where(keep, pltpu.roll(first, LANES - 16, 1), second)
             states.append(gelu(branch) + skip)
-        for polar, state in enumerate(swap(states, FIELD)):
+        for polar, state in enumerate(swap(states, FIELD, after=own_index(azimuth_count))):
             for azimuth in range(azimuth_count):
                 device = polar * azimuth_count + azimuth
                 sent[pl.ds(device * dense + tail * tile, tail), :] = state[
@@ -395,23 +402,25 @@
                 for device in range(devices)
             ],
             1,
+            begin=False,
         )
         for device in range(devices):
             state[tile, pl.ds(part * device, part), :] = blocks[device]
+    value = jnp.concatenate([state[tile] for tile in range(tiles)], axis=1)
+    center = jnp.mean(value, axis=-1, keepdims=True)
+    spread = jnp.mean((value - center) ** 2, axis=-1, keepdims=True)
+    normed = (value - center) * lax.rsqrt(spread + 1e-05) * gain[...][None, :]
+    hidden = gelu(dot(normed.astype(jnp.bfloat16), w_in[...])).astype(jnp.bfloat16)
+    size = part * lat_rows
     copies = []
     for top in range(2):
-        cells = pl.ds(top * part * lat_rows, part * lat_rows)
-        value = jnp.concatenate([state[tile, cells, :] for tile in range(tiles)], axis=1)
-        center = jnp.mean(value, axis=-1, keepdims=True)
-        spread = jnp.mean((value - center) ** 2, axis=-1, keepdims=True)
-        normed = (value - center) * lax.rsqrt(spread + 1e-05) * gain[...][None, :]
-        hidden = gelu(dot(normed.astype(jnp.bfloat16), w_in[...])).astype(jnp.bfloat16)
-        value = value + dot(hidden, w_out[...])
+        cells = slice(top * size, (top + 1) * size)
+        update = value[cells] + dot(hidden[cells], w_out[...])
         for tile in range(tiles):
-            state[tile, cells, :] = value[:, tile * LANES : (tile + 1) * LANES]
+            state[tile, cells, :] = update[:, tile * LANES : (tile + 1) * LANES]
             for lon in range(part):
                 result[top * part + lon, :, pl.ds(tile * LANES, LANES)] = state[
-                    tile, pl.ds(top * part * lat_rows + lon, lat_rows, stride=part), :
+                    tile, pl.ds(top * size + lon, lat_rows, stride=part), :
                 ]
         lons = pl.ds(top * part, part)
         copies.append(pltpu.make_async_copy(result.at[lons], mixed.at[0, lons], sems.at[top]))
@@ -482,6 +491,10 @@
         synthesise[order, 2, :, 1] = coarse[later][own]
     analyse = analyse.reshape(extra, LANES, 2 * LANES)
     synthesise = synthesise.reshape(devices, LANES, 2 * LANES)
+    for order in range(devices):
+        columns = slice(order // extra * LANES, (order // extra + 1) * LANES)
+        analyse[order % extra, :, columns] = np.roll(analyse[order % extra, :, columns], order, axis=1)
+        synthesise[order] = np.roll(synthesise[order], order, axis=0)
 
     vmem = pl.BlockSpec(memory_space=pltpu.VMEM)
     hbm = pl.BlockSpec(memory_space=pltpu.HBM)
@@ -499,7 +512,7 @@
     def far(*arrays):
         return [pltpu.with_memory_space_constraint(array, pltpu.HBM) for array in arrays]
 
-    parts = lon_cols // 8 * (channels // LANES)
+    parts = lon_cols // 8
     sent, own_filter = pl.pallas_call(
         scatter_kernel,
         in_specs=[hbm] * 3,
@@ -509,7 +522,7 @@
             pltpu.VMEM((2, degrees_here, channels, channels), jnp.float32),
         ],
         scratch_shapes=[
-            pltpu.VMEM((parts, lat_rows, 8, LANES), jnp.float32),
+            pltpu.VMEM((parts, lat_rows, 8, channels), jnp.float32),
             pltpu.SemaphoreType.DMA((parts,)),
             pltpu.SemaphoreType.DMA((2,)),
         ],

time: 87.9 us -> 86.8 us (0.987)
  Pallas kernels: 9.4 us -> 8.33 us
where the time goes in v4:
time: 86.8 us; the launch traced here: 86.6 us
  blocking collectives  78 us (90%)
  Pallas kernels  8.33 us (10%)
    all_to_all x4, blocking collectives, exchange(): moved = lax.all_to_all(split, BOTH, split_axis=0, concat_axis=0, tiled=True)  78 us
    pallas_call x1, Pallas kernels, jointly(): pl.pallas_call(scatter_kernel, in_specs=[hbm] * 3, out_specs=[vmem] * 2,...  2.04 us
    pallas_call x1, Pallas kernels, jointly(): pl.pallas_call(functools.partial(synthesis_kernel, polar_count), in_specs...  1.76 us

profile of v4, /device:TPU:0, one launch (start us, length us, event | category | flops | bytes accessed | tf_op | source)
XLA Modules:
  0.0 86.6 jit_solution(15738028200046189782)
XLA Ops:
  0.0 2.0 %scatter_channels.1 = (f32[32,24,384]{2,1,0:T(8,128)S(1)}, f32[2,2,384,384]{3,2,1,0:T(8,128)S(1)}) custom-call(f32[1,32,24,384]{3,2,1,0:T(8,128)} %field.1, f32[8,384,384]{2,1,0:T(8,128)} %real.1, f32[8,384,384]{2,1,0:T(8,128)} %imag.1), custom_call_target="tpu_custom_call" | custom-call | tf_op jit(solution)/shard_map/scatter_channels/pallas_call | solution.py:516
  2.0 0.0 copy-start.2
  2.1 0.0 copy-start.3
  2.1 0.0 copy-start.6
  2.1 0.0 copy-start.7
  2.1 37.5 %all_to_all.20.got = f32[32,24,384]{2,1,0:T(8,128)S(1)} all-to-all(f32[32,24,384]{2,1,0:T(8,128)S(1)} %get-tuple-element.9), channel_id=1, replica_groups=mesh['polar'=4,'azimuth'=8] {'polar','azimuth'}, dimensions={0} | all-to-all | bytes 2359296 | tf_op jit(solution)/shard_map/all_to_all | solution.py:506
  39.6 0.0 copy-done.2
  39.6 0.0 copy-done.3
  39.6 0.0 copy-done.6
  39.6 0.0 copy-done.7
  39.6 0.0 copy-start.1
  39.6 1.6 %analysis.1 = (f32[32,24,128]{2,1,0:T(8,128)S(1)}, f32[576,128]{1,0:T(8,128)S(1)}) custom-call(f32[32,24,384]{2,1,0:T(8,128)S(1)} %all_to_all.20.got, bf16[96,192]{1,0:T(8,128)(2,1)S(1)} %copy-done.7, bf16[96,192]{1,0:T(8,128)(2,1)S(1)} %copy-done.6, bf16[16,128,256]{2,1,0:T(8,128)(2,1)S(1)} %copy-done.3, bf16[16,128,256]{2,1,0:T(8,128)(2,1)S(1)} %copy-done.2), custom_call_target="tpu_custom_call" | custom-call | tf_op jit(solution)/shard_map/analysis/pallas_call | solution.py:533
  41.2 0.0 copy-start
  41.2 0.0 copy-start.8
  41.2 0.0 copy-start.9
  41.2 13.5 %all_to_all.21 = f32[32,9,2,128]{3,2,1,0:T(2,128)S(1)} all-to-all(f32[32,9,2,128]{3,2,1,0:T(2,128)S(1)} %bitcast.12), channel_id=1, replica_groups=mesh['polar'=4,'azimuth'=8] {'polar','azimuth'}, dimensions={0} | all-to-all | bytes 589824 | tf_op jit(solution)/shard_map/all_to_all | solution.py:506
  54.8 1.3 %channel_filter.1 = f32[576,128]{1,0:T(8,128)S(1)} custom-call(f32[576,128]{1,0:T(8,128)S(1)} %bitcast.9, f32[2,2,384,384]{3,2,1,0:T(8,128)S(1)} %get-tuple-element.11.own_filter), custom_call_target="tpu_custom_call" | custom-call | tf_op jit(solution)/shard_map/channel_filter/pallas_call | solution.py:543
  56.0 13.5 %all_to_all.22 = f32[32,9,2,128]{3,2,1,0:T(2,128)S(1)} all-to-all(f32[32,9,2,128]{3,2,1,0:T(2,128)S(1)} %bitcast.10), channel_id=1, replica_groups=mesh['polar'=4,'azimuth'=8] {'polar','azimuth'}, dimensions={0} | all-to-all | bytes 589824 | tf_op jit(solution)/shard_map/all_to_all | solution.py:506
  69.6 0.0 copy-done.1
  69.6 0.0 copy-done
  69.6 0.0 copy-done.8
  69.6 0.0 copy-done.9
  69.6 0.0 copy-start.4
  69.6 0.0 copy-start.5
  69.6 0.0 copy-start.10
  69.6 1.8 %synthesis.1 = f32[576,128]{1,0:T(8,128)S(1)} custom-call(f32[576,128]{1,0:T(8,128)S(1)} %bitcast.7, f32[32,24,128]{2,1,0:T(8,128)S(1)} %get-tuple-element.12.coef, bf16[96,96]{1,0:T(8,128)(2,1)S(1)} %copy-done.9, bf16[96,96]{1,0:T(8,128)(2,1)S(1)} %copy-done.8, bf16[32,128,256]{2,1,0:T(8,128)(2,1)S(1)} %copy-done.1, bf16[32,128,256]{2,1,0:T(8,128)(2,1)S(1)} %copy-done), custom_call_target="tpu_custom_call" | custom-call | tf_op jit(solution)/shard_map/synthesis/pallas_call | solution.py:553
  71.4 13.5 %all_to_all.23 = f32[32,9,2,128]{3,2,1,0:T(2,128)S(1)} all-to-all(f32[32,9,2,128]{3,2,1,0:T(2,128)S(1)} %bitcast.8), channel_id=1, replica_groups=mesh['polar'=4,'azimuth'=8] {'polar','azimuth'}, dimensions={0} | all-to-all | bytes 589824 | tf_op jit(solution)/shard_map/all_to_all | solution.py:506
  84.9 0.0 copy-done.4
  84.9 0.0 copy-done.5
  84.9 0.0 copy-done.10
  84.9 1.7 %mlp.1 = f32[1,12,16,384]{3,2,1,0:T(8,128)} custom-call(f32[576,128]{1,0:T(8,128)S(1)} %bitcast.11, f32[384]{0:T(512)S(1)} %copy-done.10, bf16[384,768]{1,0:T(8,128)(2,1)S(1)} %copy-done.4, bf16[768,384]{1,0:T(8,128)(2,1)S(1)} %copy-done.5), custom_call_target="tpu_custom_call" | custom-call | tf_op jit(solution)/shard_map/mlp/pallas_call | solution.py:567
Async XLA Ops:
  2.0 37.6 %copy-start.2 = (bf16[16,128,256]{2,1,0:T(8,128)(2,1)S(1)}, bf16[16,128,256]{2,1,0:T(8,128)(2,1)}, u32[]{:S(2)}) copy-start(bf16[16,128,256]{2,1,0:T(8,128)(2,1)} %constant.19.clone.leg_low) | copy-start | bytes 3145732
  2.1 37.5 %copy-start.3 = (bf16[16,128,256]{2,1,0:T(8,128)(2,1)S(1)}, bf16[16,128,256]{2,1,0:T(8,128)(2,1)}, u32[]{:S(2)}) copy-start(bf16[16,128,256]{2,1,0:T(8,128)(2,1)} %constant.18.clone.leg_high) | copy-start | bytes 3145732
  2.1 37.5 %copy-start.6 = (bf16[96,192]{1,0:T(8,128)(2,1)S(1)}, bf16[96,192]{1,0:T(8,128)(2,1)}, u32[]{:S(2)}) copy-start(bf16[96,192]{1,0:T(8,128)(2,1)} %constant.17.clone.four_low) | copy-start | bytes 110596
  2.1 37.5 %copy-start.7 = (bf16[96,192]{1,0:T(8,128)(2,1)S(1)}, bf16[96,192]{1,0:T(8,128)(2,1)}, u32[]{:S(2)}) copy-start(bf16[96,192]{1,0:T(8,128)(2,1)} %constant.16.clone.four_high) | copy-start | bytes 110596
  39.6 29.9 %copy-start.1 = (bf16[32,128,256]{2,1,0:T(8,128)(2,1)S(1)}, bf16[32,128,256]{2,1,0:T(8,128)(2,1)}, u32[]{:S(2)}) copy-start(bf16[32,128,256]{2,1,0:T(8,128)(2,1)} %constant.22.clone.leg_high) | copy-start | bytes 6291460
  41.2 28.4 %copy-start = (bf16[32,128,256]{2,1,0:T(8,128)(2,1)S(1)}, bf16[32,128,256]{2,1,0:T(8,128)(2,1)}, u32[]{:S(2)}) copy-start(bf16[32,128,256]{2,1,0:T(8,128)(2,1)} %constant.23.clone.leg_low) | copy-start | bytes 6291460
  41.2 28.3 %copy-start.8 = (bf16[96,96]{1,0:T(8,128)(2,1)S(1)}, bf16[96,96]{1,0:T(8,128)(2,1)}, u32[]{:S(2)}) copy-start(bf16[96,96]{1,0:T(8,128)(2,1)} %constant.21.clone.four_low) | copy-start | bytes 55300
  41.2 28.3 %copy-start.9 = (bf16[96,96]{1,0:T(8,128)(2,1)S(1)}, bf16[96,96]{1,0:T(8,128)(2,1)}, u32[]{:S(2)}) copy-start(bf16[96,96]{1,0:T(8,128)(2,1)} %constant.20.clone.four_high) | copy-start | bytes 55300
  69.6 15.3 %copy-start.4 = (bf16[384,768]{1,0:T(8,128)(2,1)S(1)}, bf16[384,768]{1,0:T(8,128)(2,1)}, u32[]{:S(2)}) copy-start(bf16[384,768]{1,0:T(8,128)(2,1)} %w_in.1) | copy-start | bytes 1769476
  69.6 15.3 %copy-start.5 = (bf16[768,384]{1,0:T(8,128)(2,1)S(1)}, bf16[768,384]{1,0:T(8,128)(2,1)}, u32[]{:S(2)}) copy-start(bf16[768,384]{1,0:T(8,128)(2,1)} %w_out.1) | copy-start | bytes 1769476
  69.6 15.3 %copy-start.10 = (f32[384]{0:T(512)S(1)}, f32[384]{0:T(512)}, u32[]{:S(2)}) copy-start(f32[384]{0:T(512)} %gain.1) | copy-start | bytes 4612

commit v5 on v4

--- a/solution.py
+++ b/solution.py
@@ -545,7 +545,7 @@
         in_specs=[vmem] * 2,
         out_specs=vmem,
         out_shape=block,
-        scratch_shapes=[pltpu.VMEM((devices * dense, LANES), jnp.float32)],
+        scratch_shapes=[pltpu.VMEM((devices * count, LANES), jnp.float32)],
         compiler_params=pltpu.CompilerParams(vmem_limit_bytes=8 * MIB),
         name="channel_filter",
     )(*near(got, own_filter))

time: 86.8 us -> 86.8 us (level)
  no operation moved by 1% of the time
where the time goes in v5:
time: 86.8 us; the launch traced here: 86.6 us
  blocking collectives  78 us (90%)
  Pallas kernels  8.33 us (10%)
    all_to_all x4, blocking collectives, exchange(): moved = lax.all_to_all(split, BOTH, split_axis=0, concat_axis=0, tiled=True)  78 us
    pallas_call x1, Pallas kernels, jointly(): pl.pallas_call(scatter_kernel, in_specs=[hbm] * 3, out_specs=[vmem] * 2,...  2.04 us
    pallas_call x1, Pallas kernels, jointly(): pl.pallas_call(functools.partial(synthesis_kernel, polar_count), in_specs...  1.76 us

profile of v5, /device:TPU:0, one launch (start us, length us, event | category | flops | bytes accessed | tf_op | source)
XLA Modules:
  0.0 86.6 jit_solution(12138417814851281696)
XLA Ops:
  0.0 2.0 %scatter_channels.1 = (f32[32,24,384]{2,1,0:T(8,128)S(1)}, f32[2,2,384,384]{3,2,1,0:T(8,128)S(1)}) custom-call(f32[1,32,24,384]{3,2,1,0:T(8,128)} %field.1, f32[8,384,384]{2,1,0:T(8,128)} %real.1, f32[8,384,384]{2,1,0:T(8,128)} %imag.1), custom_call_target="tpu_custom_call" | custom-call | tf_op jit(solution)/shard_map/scatter_channels/pallas_call | solution.py:516
  2.0 0.0 copy-start.2
  2.1 0.0 copy-start.3
  2.1 0.0 copy-start.6
  2.1 0.0 copy-start.7
  2.1 37.5 %all_to_all.20.got = f32[32,24,384]{2,1,0:T(8,128)S(1)} all-to-all(f32[32,24,384]{2,1,0:T(8,128)S(1)} %get-tuple-element.9), channel_id=1, replica_groups=mesh['polar'=4,'azimuth'=8] {'polar','azimuth'}, dimensions={0} | all-to-all | bytes 2359296 | tf_op jit(solution)/shard_map/all_to_all | solution.py:506
  39.6 0.0 copy-done.2
  39.6 0.0 copy-done.3
  39.6 0.0 copy-done.6
  39.6 0.0 copy-done.7
  39.6 0.0 copy-start.1
  39.6 1.6 %analysis.1 = (f32[32,24,128]{2,1,0:T(8,128)S(1)}, f32[576,128]{1,0:T(8,128)S(1)}) custom-call(f32[32,24,384]{2,1,0:T(8,128)S(1)} %all_to_all.20.got, bf16[96,192]{1,0:T(8,128)(2,1)S(1)} %copy-done.7, bf16[96,192]{1,0:T(8,128)(2,1)S(1)} %copy-done.6, bf16[16,128,256]{2,1,0:T(8,128)(2,1)S(1)} %copy-done.3, bf16[16,128,256]{2,1,0:T(8,128)(2,1)S(1)} %copy-done.2), custom_call_target="tpu_custom_call" | custom-call | tf_op jit(solution)/shard_map/analysis/pallas_call | solution.py:533
  41.2 0.0 copy-start
  41.2 0.0 copy-start.8
  41.2 0.0 copy-start.9
  41.2 13.5 %all_to_all.21 = f32[32,9,2,128]{3,2,1,0:T(2,128)S(1)} all-to-all(f32[32,9,2,128]{3,2,1,0:T(2,128)S(1)} %bitcast.12), channel_id=1, replica_groups=mesh['polar'=4,'azimuth'=8] {'polar','azimuth'}, dimensions={0} | all-to-all | bytes 589824 | tf_op jit(solution)/shard_map/all_to_all | solution.py:506
  54.8 1.3 %channel_filter.1 = f32[576,128]{1,0:T(8,128)S(1)} custom-call(f32[576,128]{1,0:T(8,128)S(1)} %bitcast.9, f32[2,2,384,384]{3,2,1,0:T(8,128)S(1)} %get-tuple-element.11.own_filter), custom_call_target="tpu_custom_call" | custom-call | tf_op jit(solution)/shard_map/channel_filter/pallas_call | solution.py:543
  56.0 13.5 %all_to_all.22 = f32[32,9,2,128]{3,2,1,0:T(2,128)S(1)} all-to-all(f32[32,9,2,128]{3,2,1,0:T(2,128)S(1)} %bitcast.10), channel_id=1, replica_groups=mesh['polar'=4,'azimuth'=8] {'polar','azimuth'}, dimensions={0} | all-to-all | bytes 589824 | tf_op jit(solution)/shard_map/all_to_all | solution.py:506
  69.6 0.0 copy-done.1
  69.6 0.0 copy-done
  69.6 0.0 copy-done.8
  69.6 0.0 copy-done.9
  69.6 0.0 copy-start.4
  69.6 0.0 copy-start.5
  69.6 0.0 copy-start.10
  69.6 1.8 %synthesis.1 = f32[576,128]{1,0:T(8,128)S(1)} custom-call(f32[576,128]{1,0:T(8,128)S(1)} %bitcast.7, f32[32,24,128]{2,1,0:T(8,128)S(1)} %get-tuple-element.12.coef, bf16[96,96]{1,0:T(8,128)(2,1)S(1)} %copy-done.9, bf16[96,96]{1,0:T(8,128)(2,1)S(1)} %copy-done.8, bf16[32,128,256]{2,1,0:T(8,128)(2,1)S(1)} %copy-done.1, bf16[32,128,256]{2,1,0:T(8,128)(2,1)S(1)} %copy-done), custom_call_target="tpu_custom_call" | custom-call | tf_op jit(solution)/shard_map/synthesis/pallas_call | solution.py:553
  71.4 13.5 %all_to_all.23 = f32[32,9,2,128]{3,2,1,0:T(2,128)S(1)} all-to-all(f32[32,9,2,128]{3,2,1,0:T(2,128)S(1)} %bitcast.8), channel_id=1, replica_groups=mesh['polar'=4,'azimuth'=8] {'polar','azimuth'}, dimensions={0} | all-to-all | bytes 589824 | tf_op jit(solution)/shard_map/all_to_all | solution.py:506
  84.9 0.0 copy-done.4
  84.9 0.0 copy-done.5
  84.9 0.0 copy-done.10
  84.9 1.7 %mlp.1 = f32[1,12,16,384]{3,2,1,0:T(8,128)} custom-call(f32[576,128]{1,0:T(8,128)S(1)} %bitcast.11, f32[384]{0:T(512)S(1)} %copy-done.10, bf16[384,768]{1,0:T(8,128)(2,1)S(1)} %copy-done.4, bf16[768,384]{1,0:T(8,128)(2,1)S(1)} %copy-done.5), custom_call_target="tpu_custom_call" | custom-call | tf_op jit(solution)/shard_map/mlp/pallas_call | solution.py:567
Async XLA Ops:
  2.0 37.6 %copy-start.2 = (bf16[16,128,256]{2,1,0:T(8,128)(2,1)S(1)}, bf16[16,128,256]{2,1,0:T(8,128)(2,1)}, u32[]{:S(2)}) copy-start(bf16[16,128,256]{2,1,0:T(8,128)(2,1)} %constant.19.clone.leg_low) | copy-start | bytes 3145732
  2.1 37.5 %copy-start.3 = (bf16[16,128,256]{2,1,0:T(8,128)(2,1)S(1)}, bf16[16,128,256]{2,1,0:T(8,128)(2,1)}, u32[]{:S(2)}) copy-start(bf16[16,128,256]{2,1,0:T(8,128)(2,1)} %constant.18.clone.leg_high) | copy-start | bytes 3145732
  2.1 37.5 %copy-start.6 = (bf16[96,192]{1,0:T(8,128)(2,1)S(1)}, bf16[96,192]{1,0:T(8,128)(2,1)}, u32[]{:S(2)}) copy-start(bf16[96,192]{1,0:T(8,128)(2,1)} %constant.17.clone.four_low) | copy-start | bytes 110596
  2.1 37.5 %copy-start.7 = (bf16[96,192]{1,0:T(8,128)(2,1)S(1)}, bf16[96,192]{1,0:T(8,128)(2,1)}, u32[]{:S(2)}) copy-start(bf16[96,192]{1,0:T(8,128)(2,1)} %constant.16.clone.four_high) | copy-start | bytes 110596
  39.6 29.9 %copy-start.1 = (bf16[32,128,256]{2,1,0:T(8,128)(2,1)S(1)}, bf16[32,128,256]{2,1,0:T(8,128)(2,1)}, u32[]{:S(2)}) copy-start(bf16[32,128,256]{2,1,0:T(8,128)(2,1)} %constant.22.clone.leg_high) | copy-start | bytes 6291460
  41.2 28.4 %copy-start = (bf16[32,128,256]{2,1,0:T(8,128)(2,1)S(1)}, bf16[32,128,256]{2,1,0:T(8,128)(2,1)}, u32[]{:S(2)}) copy-start(bf16[32,128,256]{2,1,0:T(8,128)(2,1)} %constant.23.clone.leg_low) | copy-start | bytes 6291460
  41.2 28.3 %copy-start.8 = (bf16[96,96]{1,0:T(8,128)(2,1)S(1)}, bf16[96,96]{1,0:T(8,128)(2,1)}, u32[]{:S(2)}) copy-start(bf16[96,96]{1,0:T(8,128)(2,1)} %constant.21.clone.four_low) | copy-start | bytes 55300
  41.2 28.3 %copy-start.9 = (bf16[96,96]{1,0:T(8,128)(2,1)S(1)}, bf16[96,96]{1,0:T(8,128)(2,1)}, u32[]{:S(2)}) copy-start(bf16[96,96]{1,0:T(8,128)(2,1)} %constant.20.clone.four_high) | copy-start | bytes 55300
  69.6 15.3 %copy-start.4 = (bf16[384,768]{1,0:T(8,128)(2,1)S(1)}, bf16[384,768]{1,0:T(8,128)(2,1)}, u32[]{:S(2)}) copy-start(bf16[384,768]{1,0:T(8,128)(2,1)} %w_in.1) | copy-start | bytes 1769476
  69.6 15.3 %copy-start.5 = (bf16[768,384]{1,0:T(8,128)(2,1)S(1)}, bf16[768,384]{1,0:T(8,128)(2,1)}, u32[]{:S(2)}) copy-start(bf16[768,384]{1,0:T(8,128)(2,1)} %w_out.1) | copy-start | bytes 1769476
  69.6 15.3 %copy-start.10 = (f32[384]{0:T(512)S(1)}, f32[384]{0:T(512)}, u32[]{:S(2)}) copy-start(f32[384]{0:T(512)} %gain.1) | copy-start | bytes 4612

commit v6 on v5

--- a/solution.py
+++ b/solution.py
@@ -215,12 +215,17 @@
     four = jnp.concatenate([four_high[...], four_low[...]], axis=0)
     tiles = width // LANES
     own_turn = LANES - own_index(azimuth_count)
-    wide = []
-    for polar in range(polar_count):
-        block = got[pl.ds(polar * azimuth_count, azimuth_count)]
-        block_high, block_low = split_bf16(block.reshape(azimuth_count * lon_cols, width))
-        both = dot(four, block_high)
-        wide.append(both[:modes] + both[modes:] + dot(four[:modes], block_low))
+    block = jnp.concatenate(
+        [
+            got[pl.ds(polar * azimuth_count, azimuth_count)].reshape(azimuth_count * lon_cols, width)
+            for polar in range(polar_count)
+        ],
+        axis=1,
+    )
+    block_high, block_low = split_bf16(block)
+    both = dot(four, block_high)
+    both = both[:modes] + both[modes:] + dot(four[:modes], block_low)
+    wide = [both[:, polar * width : (polar + 1) * width] for polar in range(polar_count)]
     for tile in range(tiles):
         spectra = [spectrum[:, tile * LANES : (tile + 1) * LANES] for spectrum in wide]
         for quad, spectrum in enumerate(swap(spectra, FIELD, before=own_turn)):
@@ -369,16 +374,26 @@
     half = points // 2
     keep = (lax.broadcasted_iota(jnp.int32, (half, LANES), 1) & 16) == 0
     for tile in range(count // 8):
+        modes = jnp.concatenate(
+            [
+                jnp.concatenate(
+                    [
+                        modes_buf[pl.ds(2 * (QUAD * tile + quad) + part, orders, stride=count), :]
+                        for part in range(2)
+                    ],
+                    axis=0,
+                )
+                for quad in range(QUAD)
+            ],
+            axis=1,
+        )
+        modes_high, modes_low = split_bf16(modes)
+        both = dot(four, modes_high)
+        values = both[:points] + both[points:] + dot(four[:points], modes_low)
         states = []
-        for quad in range(4):
-            row = 2 * (4 * tile + quad)
-            modes = jnp.concatenate(
-                [modes_buf[pl.ds(row + part, orders, stride=count), :] for part in range(2)], axis=0
-            )
-            modes_high, modes_low = split_bf16(modes)
-            both = dot(four, modes_high)
-            values = both[:points] + both[points:] + dot(four[:points], modes_low)
-            first, second = values[:half], values[half:]
+        for quad in range(QUAD):
+            lanes = slice(quad * LANES, (quad + 1) * LANES)
+            first, second = values[:half, lanes], values[half:, lanes]
             skip = jnp.where(keep, first, pltpu.roll(second, 16, 1))
             branch = jnp.where(keep, pltpu.roll(first, LANES - 16, 1), second)
             states.append(gelu(branch) + skip)

time: 86.8 us -> 86.7 us (level)
  no operation moved by 1% of the time
where the time goes in v6:
time: 86.7 us; the launch traced here: 86.5 us
  blocking collectives  78 us (90%)
  Pallas kernels  8.28 us (10%)
    all_to_all x4, blocking collectives, exchange(): moved = lax.all_to_all(split, BOTH, split_axis=0, concat_axis=0, tiled=True)  78 us
    pallas_call x1, Pallas kernels, jointly(): pl.pallas_call(scatter_kernel, in_specs=[hbm] * 3, out_specs=[vmem] * 2,...  2.04 us
    pallas_call x1, Pallas kernels, jointly(): pl.pallas_call(functools.partial(synthesis_kernel, polar_count), in_specs...  1.76 us

profile of v6, /device:TPU:0, one launch (start us, length us, event | category | flops | bytes accessed | tf_op | source)
XLA Modules:
  0.0 86.5 jit_solution(10238532357260599573)
XLA Ops:
  0.0 2.0 %scatter_channels.1 = (f32[32,24,384]{2,1,0:T(8,128)S(1)}, f32[2,2,384,384]{3,2,1,0:T(8,128)S(1)}) custom-call(f32[1,32,24,384]{3,2,1,0:T(8,128)} %field.1, f32[8,384,384]{2,1,0:T(8,128)} %real.1, f32[8,384,384]{2,1,0:T(8,128)} %imag.1), custom_call_target="tpu_custom_call" | custom-call | tf_op jit(solution)/shard_map/scatter_channels/pallas_call | solution.py:531
  2.0 0.0 copy-start.2
  2.1 0.0 copy-start.3
  2.1 0.0 copy-start.6
  2.1 0.0 copy-start.7
  2.1 37.5 %all_to_all.20.got = f32[32,24,384]{2,1,0:T(8,128)S(1)} all-to-all(f32[32,24,384]{2,1,0:T(8,128)S(1)} %get-tuple-element.9), channel_id=1, replica_groups=mesh['polar'=4,'azimuth'=8] {'polar','azimuth'}, dimensions={0} | all-to-all | bytes 2359296 | tf_op jit(solution)/shard_map/all_to_all | solution.py:521
  39.6 0.0 copy-done.2
  39.6 0.0 copy-done.3
  39.6 0.0 copy-done.6
  39.6 0.0 copy-done.7
  39.6 0.0 copy-start.1
  39.6 1.5 %analysis.1 = (f32[32,24,128]{2,1,0:T(8,128)S(1)}, f32[576,128]{1,0:T(8,128)S(1)}) custom-call(f32[32,24,384]{2,1,0:T(8,128)S(1)} %all_to_all.20.got, bf16[96,192]{1,0:T(8,128)(2,1)S(1)} %copy-done.7, bf16[96,192]{1,0:T(8,128)(2,1)S(1)} %copy-done.6, bf16[16,128,256]{2,1,0:T(8,128)(2,1)S(1)} %copy-done.3, bf16[16,128,256]{2,1,0:T(8,128)(2,1)S(1)} %copy-done.2), custom_call_target="tpu_custom_call" | custom-call | tf_op jit(solution)/shard_map/analysis/pallas_call | solution.py:548
  41.2 0.0 copy-start
  41.2 0.0 copy-start.8
  41.2 0.0 copy-start.9
  41.2 13.5 %all_to_all.21 = f32[32,9,2,128]{3,2,1,0:T(2,128)S(1)} all-to-all(f32[32,9,2,128]{3,2,1,0:T(2,128)S(1)} %bitcast.12), channel_id=1, replica_groups=mesh['polar'=4,'azimuth'=8] {'polar','azimuth'}, dimensions={0} | all-to-all | bytes 589824 | tf_op jit(solution)/shard_map/all_to_all | solution.py:521
  54.7 1.3 %channel_filter.1 = f32[576,128]{1,0:T(8,128)S(1)} custom-call(f32[576,128]{1,0:T(8,128)S(1)} %bitcast.9, f32[2,2,384,384]{3,2,1,0:T(8,128)S(1)} %get-tuple-element.11.own_filter), custom_call_target="tpu_custom_call" | custom-call | tf_op jit(solution)/shard_map/channel_filter/pallas_call | solution.py:558
  56.0 13.5 %all_to_all.22 = f32[32,9,2,128]{3,2,1,0:T(2,128)S(1)} all-to-all(f32[32,9,2,128]{3,2,1,0:T(2,128)S(1)} %bitcast.10), channel_id=1, replica_groups=mesh['polar'=4,'azimuth'=8] {'polar','azimuth'}, dimensions={0} | all-to-all | bytes 589824 | tf_op jit(solution)/shard_map/all_to_all | solution.py:521
  69.5 0.0 copy-done.1
  69.5 0.0 copy-done
  69.5 0.0 copy-done.8
  69.5 0.0 copy-done.9
  69.5 0.0 copy-start.4
  69.5 0.0 copy-start.5
  69.5 0.0 copy-start.10
  69.5 1.8 %synthesis.1 = f32[576,128]{1,0:T(8,128)S(1)} custom-call(f32[576,128]{1,0:T(8,128)S(1)} %bitcast.7, f32[32,24,128]{2,1,0:T(8,128)S(1)} %get-tuple-element.12.coef, bf16[96,96]{1,0:T(8,128)(2,1)S(1)} %copy-done.9, bf16[96,96]{1,0:T(8,128)(2,1)S(1)} %copy-done.8, bf16[32,128,256]{2,1,0:T(8,128)(2,1)S(1)} %copy-done.1, bf16[32,128,256]{2,1,0:T(8,128)(2,1)S(1)} %copy-done), custom_call_target="tpu_custom_call" | custom-call | tf_op jit(solution)/shard_map/synthesis/pallas_call | solution.py:568
  71.3 13.5 %all_to_all.23 = f32[32,9,2,128]{3,2,1,0:T(2,128)S(1)} all-to-all(f32[32,9,2,128]{3,2,1,0:T(2,128)S(1)} %bitcast.8), channel_id=1, replica_groups=mesh['polar'=4,'azimuth'=8] {'polar','azimuth'}, dimensions={0} | all-to-all | bytes 589824 | tf_op jit(solution)/shard_map/all_to_all | solution.py:521
  84.8 0.0 copy-done.4
  84.8 0.0 copy-done.5
  84.8 0.0 copy-done.10
  84.8 1.7 %mlp.1 = f32[1,12,16,384]{3,2,1,0:T(8,128)} custom-call(f32[576,128]{1,0:T(8,128)S(1)} %bitcast.11, f32[384]{0:T(512)S(1)} %copy-done.10, bf16[384,768]{1,0:T(8,128)(2,1)S(1)} %copy-done.4, bf16[768,384]{1,0:T(8,128)(2,1)S(1)} %copy-done.5), custom_call_target="tpu_custom_call" | custom-call | tf_op jit(solution)/shard_map/mlp/pallas_call | solution.py:582
Async XLA Ops:
  2.0 37.6 %copy-start.2 = (bf16[16,128,256]{2,1,0:T(8,128)(2,1)S(1)}, bf16[16,128,256]{2,1,0:T(8,128)(2,1)}, u32[]{:S(2)}) copy-start(bf16[16,128,256]{2,1,0:T(8,128)(2,1)} %constant.19.clone.leg_low) | copy-start | bytes 3145732
  2.1 37.5 %copy-start.3 = (bf16[16,128,256]{2,1,0:T(8,128)(2,1)S(1)}, bf16[16,128,256]{2,1,0:T(8,128)(2,1)}, u32[]{:S(2)}) copy-start(bf16[16,128,256]{2,1,0:T(8,128)(2,1)} %constant.18.clone.leg_high) | copy-start | bytes 3145732
  2.1 37.5 %copy-start.6 = (bf16[96,192]{1,0:T(8,128)(2,1)S(1)}, bf16[96,192]{1,0:T(8,128)(2,1)}, u32[]{:S(2)}) copy-start(bf16[96,192]{1,0:T(8,128)(2,1)} %constant.17.clone.four_low) | copy-start | bytes 110596
  2.1 37.5 %copy-start.7 = (bf16[96,192]{1,0:T(8,128)(2,1)S(1)}, bf16[96,192]{1,0:T(8,128)(2,1)}, u32[]{:S(2)}) copy-start(bf16[96,192]{1,0:T(8,128)(2,1)} %constant.16.clone.four_high) | copy-start | bytes 110596
  39.6 29.9 %copy-start.1 = (bf16[32,128,256]{2,1,0:T(8,128)(2,1)S(1)}, bf16[32,128,256]{2,1,0:T(8,128)(2,1)}, u32[]{:S(2)}) copy-start(bf16[32,128,256]{2,1,0:T(8,128)(2,1)} %constant.22.clone.leg_high) | copy-start | bytes 6291460
  41.2 28.3 %copy-start = (bf16[32,128,256]{2,1,0:T(8,128)(2,1)S(1)}, bf16[32,128,256]{2,1,0:T(8,128)(2,1)}, u32[]{:S(2)}) copy-start(bf16[32,128,256]{2,1,0:T(8,128)(2,1)} %constant.23.clone.leg_low) | copy-start | bytes 6291460
  41.2 28.3 %copy-start.8 = (bf16[96,96]{1,0:T(8,128)(2,1)S(1)}, bf16[96,96]{1,0:T(8,128)(2,1)}, u32[]{:S(2)}) copy-start(bf16[96,96]{1,0:T(8,128)(2,1)} %constant.21.clone.four_low) | copy-start | bytes 55300
  41.2 28.3 %copy-start.9 = (bf16[96,96]{1,0:T(8,128)(2,1)S(1)}, bf16[96,96]{1,0:T(8,128)(2,1)}, u32[]{:S(2)}) copy-start(bf16[96,96]{1,0:T(8,128)(2,1)} %constant.20.clone.four_high) | copy-start | bytes 55300
  69.5 15.3 %copy-start.4 = (bf16[384,768]{1,0:T(8,128)(2,1)S(1)}, bf16[384,768]{1,0:T(8,128)(2,1)}, u32[]{:S(2)}) copy-start(bf16[384,768]{1,0:T(8,128)(2,1)} %w_in.1) | copy-start | bytes 1769476
  69.5 15.3 %copy-start.5 = (bf16[768,384]{1,0:T(8,128)(2,1)S(1)}, bf16[768,384]{1,0:T(8,128)(2,1)}, u32[]{:S(2)}) copy-start(bf16[768,384]{1,0:T(8,128)(2,1)} %w_out.1) | copy-start | bytes 1769476
  69.5 15.3 %copy-start.10 = (f32[384]{0:T(512)S(1)}, f32[384]{0:T(512)}, u32[]{:S(2)}) copy-start(f32[384]{0:T(512)} %gain.1) | copy-start | bytes 4612

commit v7 on v6

--- a/solution.py
+++ b/solution.py
@@ -186,11 +186,15 @@
         copies.append(copy)
     degrees = own_filter.shape[1]
     start = lax.axis_index("polar") * degrees
+    size = channels // 2
     filter_copies = [
         pltpu.make_async_copy(
-            part.at[pl.ds(start, degrees)], own_filter.at[index], filter_sems.at[index]
+            part.at[pl.ds(start, degrees), pl.ds(piece * size, size)],
+            own_filter.at[index, :, pl.ds(piece * size, size)],
+            filter_sems.at[index, piece],
         )
         for index, part in enumerate((real, imag))
+        for piece in range(2)
     ]
     for copy in filter_copies:
         copy.start()
@@ -539,7 +543,7 @@
         scratch_shapes=[
             pltpu.VMEM((parts, lat_rows, 8, channels), jnp.float32),
             pltpu.SemaphoreType.DMA((parts,)),
-            pltpu.SemaphoreType.DMA((2,)),
+            pltpu.SemaphoreType.DMA((2, 2)),
         ],
         compiler_params=pltpu.CompilerParams(vmem_limit_bytes=8 * MIB),
         name="scatter_channels",

time: 86.7 us -> 86.7 us (level)
  no operation moved by 1% of the time
where the time goes in v7:
time: 86.7 us; the launch traced here: 86.5 us
  blocking collectives  78 us (90%)
  Pallas kernels  8.25 us (10%)
    all_to_all x4, blocking collectives, exchange(): moved = lax.all_to_all(split, BOTH, split_axis=0, concat_axis=0, tiled=True)  78 us
    pallas_call x1, Pallas kernels, jointly(): pl.pallas_call(scatter_kernel, in_specs=[hbm] * 3, out_specs=[vmem] * 2,...  2.02 us
    pallas_call x1, Pallas kernels, jointly(): pl.pallas_call(functools.partial(synthesis_kernel, polar_count), in_specs...  1.76 us

profile of v7, /device:TPU:0, one launch (start us, length us, event | category | flops | bytes accessed | tf_op | source)
XLA Modules:
  0.0 86.5 jit_solution(5125677624604720329)
XLA Ops:
  0.0 2.0 %scatter_channels.1 = (f32[32,24,384]{2,1,0:T(8,128)S(1)}, f32[2,2,384,384]{3,2,1,0:T(8,128)S(1)}) custom-call(f32[1,32,24,384]{3,2,1,0:T(8,128)} %field.1, f32[8,384,384]{2,1,0:T(8,128)} %real.1, f32[8,384,384]{2,1,0:T(8,128)} %imag.1), custom_call_target="tpu_custom_call" | custom-call | tf_op jit(solution)/shard_map/scatter_channels/pallas_call | solution.py:535
  2.0 0.0 copy-start.2
  2.0 0.0 copy-start.3
  2.1 0.0 copy-start.6
  2.1 0.0 copy-start.7
  2.1 37.5 %all_to_all.20.got = f32[32,24,384]{2,1,0:T(8,128)S(1)} all-to-all(f32[32,24,384]{2,1,0:T(8,128)S(1)} %get-tuple-element.9), channel_id=1, replica_groups=mesh['polar'=4,'azimuth'=8] {'polar','azimuth'}, dimensions={0} | all-to-all | bytes 2359296 | tf_op jit(solution)/shard_map/all_to_all | solution.py:525
  39.6 0.0 copy-done.2
  39.6 0.0 copy-done.3
  39.6 0.0 copy-done.6
  39.6 0.0 copy-done.7
  39.6 0.0 copy-start.1
  39.6 1.5 %analysis.1 = (f32[32,24,128]{2,1,0:T(8,128)S(1)}, f32[576,128]{1,0:T(8,128)S(1)}) custom-call(f32[32,24,384]{2,1,0:T(8,128)S(1)} %all_to_all.20.got, bf16[96,192]{1,0:T(8,128)(2,1)S(1)} %copy-done.7, bf16[96,192]{1,0:T(8,128)(2,1)S(1)} %copy-done.6, bf16[16,128,256]{2,1,0:T(8,128)(2,1)S(1)} %copy-done.3, bf16[16,128,256]{2,1,0:T(8,128)(2,1)S(1)} %copy-done.2), custom_call_target="tpu_custom_call" | custom-call | tf_op jit(solution)/shard_map/analysis/pallas_call | solution.py:552
  41.1 0.0 copy-start
  41.1 0.0 copy-start.8
  41.2 0.0 copy-start.9
  41.2 13.5 %all_to_all.21 = f32[32,9,2,128]{3,2,1,0:T(2,128)S(1)} all-to-all(f32[32,9,2,128]{3,2,1,0:T(2,128)S(1)} %bitcast.12), channel_id=1, replica_groups=mesh['polar'=4,'azimuth'=8] {'polar','azimuth'}, dimensions={0} | all-to-all | bytes 589824 | tf_op jit(solution)/shard_map/all_to_all | solution.py:525
  54.7 1.3 %channel_filter.1 = f32[576,128]{1,0:T(8,128)S(1)} custom-call(f32[576,128]{1,0:T(8,128)S(1)} %bitcast.9, f32[2,2,384,384]{3,2,1,0:T(8,128)S(1)} %get-tuple-element.11.own_filter), custom_call_target="tpu_custom_call" | custom-call | tf_op jit(solution)/shard_map/channel_filter/pallas_call | solution.py:562
  56.0 13.5 %all_to_all.22 = f32[32,9,2,128]{3,2,1,0:T(2,128)S(1)} all-to-all(f32[32,9,2,128]{3,2,1,0:T(2,128)S(1)} %bitcast.10), channel_id=1, replica_groups=mesh['polar'=4,'azimuth'=8] {'polar','azimuth'}, dimensions={0} | all-to-all | bytes 589824 | tf_op jit(solution)/shard_map/all_to_all | solution.py:525
  69.5 0.0 copy-done.1
  69.5 0.0 copy-done
  69.5 0.0 copy-done.8
  69.5 0.0 copy-done.9
  69.5 0.0 copy-start.4
  69.5 0.0 copy-start.5
  69.5 0.0 copy-start.10
  69.5 1.8 %synthesis.1 = f32[576,128]{1,0:T(8,128)S(1)} custom-call(f32[576,128]{1,0:T(8,128)S(1)} %bitcast.7, f32[32,24,128]{2,1,0:T(8,128)S(1)} %get-tuple-element.12.coef, bf16[96,96]{1,0:T(8,128)(2,1)S(1)} %copy-done.9, bf16[96,96]{1,0:T(8,128)(2,1)S(1)} %copy-done.8, bf16[32,128,256]{2,1,0:T(8,128)(2,1)S(1)} %copy-done.1, bf16[32,128,256]{2,1,0:T(8,128)(2,1)S(1)} %copy-done), custom_call_target="tpu_custom_call" | custom-call | tf_op jit(solution)/shard_map/synthesis/pallas_call | solution.py:572
  71.3 13.5 %all_to_all.23 = f32[32,9,2,128]{3,2,1,0:T(2,128)S(1)} all-to-all(f32[32,9,2,128]{3,2,1,0:T(2,128)S(1)} %bitcast.8), channel_id=1, replica_groups=mesh['polar'=4,'azimuth'=8] {'polar','azimuth'}, dimensions={0} | all-to-all | bytes 589824 | tf_op jit(solution)/shard_map/all_to_all | solution.py:525
  84.8 0.0 copy-done.4
  84.8 0.0 copy-done.5
  84.8 0.0 copy-done.10
  84.8 1.7 %mlp.1 = f32[1,12,16,384]{3,2,1,0:T(8,128)} custom-call(f32[576,128]{1,0:T(8,128)S(1)} %bitcast.11, f32[384]{0:T(512)S(1)} %copy-done.10, bf16[384,768]{1,0:T(8,128)(2,1)S(1)} %copy-done.4, bf16[768,384]{1,0:T(8,128)(2,1)S(1)} %copy-done.5), custom_call_target="tpu_custom_call" | custom-call | tf_op jit(solution)/shard_map/mlp/pallas_call | solution.py:586
Async XLA Ops:
  2.0 37.6 %copy-start.2 = (bf16[16,128,256]{2,1,0:T(8,128)(2,1)S(1)}, bf16[16,128,256]{2,1,0:T(8,128)(2,1)}, u32[]{:S(2)}) copy-start(bf16[16,128,256]{2,1,0:T(8,128)(2,1)} %constant.19.clone.leg_low) | copy-start | bytes 3145732
  2.0 37.5 %copy-start.3 = (bf16[16,128,256]{2,1,0:T(8,128)(2,1)S(1)}, bf16[16,128,256]{2,1,0:T(8,128)(2,1)}, u32[]{:S(2)}) copy-start(bf16[16,128,256]{2,1,0:T(8,128)(2,1)} %constant.18.clone.leg_high) | copy-start | bytes 3145732
  2.1 37.5 %copy-start.6 = (bf16[96,192]{1,0:T(8,128)(2,1)S(1)}, bf16[96,192]{1,0:T(8,128)(2,1)}, u32[]{:S(2)}) copy-start(bf16[96,192]{1,0:T(8,128)(2,1)} %constant.17.clone.four_low) | copy-start | bytes 110596
  2.1 37.5 %copy-start.7 = (bf16[96,192]{1,0:T(8,128)(2,1)S(1)}, bf16[96,192]{1,0:T(8,128)(2,1)}, u32[]{:S(2)}) copy-start(bf16[96,192]{1,0:T(8,128)(2,1)} %constant.16.clone.four_high) | copy-start | bytes 110596
  39.6 29.9 %copy-start.1 = (bf16[32,128,256]{2,1,0:T(8,128)(2,1)S(1)}, bf16[32,128,256]{2,1,0:T(8,128)(2,1)}, u32[]{:S(2)}) copy-start(bf16[32,128,256]{2,1,0:T(8,128)(2,1)} %constant.22.clone.leg_high) | copy-start | bytes 6291460
  41.1 28.3 %copy-start = (bf16[32,128,256]{2,1,0:T(8,128)(2,1)S(1)}, bf16[32,128,256]{2,1,0:T(8,128)(2,1)}, u32[]{:S(2)}) copy-start(bf16[32,128,256]{2,1,0:T(8,128)(2,1)} %constant.23.clone.leg_low) | copy-start | bytes 6291460
  41.1 28.3 %copy-start.8 = (bf16[96,96]{1,0:T(8,128)(2,1)S(1)}, bf16[96,96]{1,0:T(8,128)(2,1)}, u32[]{:S(2)}) copy-start(bf16[96,96]{1,0:T(8,128)(2,1)} %constant.21.clone.four_low) | copy-start | bytes 55300
  41.2 28.3 %copy-start.9 = (bf16[96,96]{1,0:T(8,128)(2,1)S(1)}, bf16[96,96]{1,0:T(8,128)(2,1)}, u32[]{:S(2)}) copy-start(bf16[96,96]{1,0:T(8,128)(2,1)} %constant.20.clone.four_high) | copy-start | bytes 55300
  69.5 15.3 %copy-start.4 = (bf16[384,768]{1,0:T(8,128)(2,1)S(1)}, bf16[384,768]{1,0:T(8,128)(2,1)}, u32[]{:S(2)}) copy-start(bf16[384,768]{1,0:T(8,128)(2,1)} %w_in.1) | copy-start | bytes 1769476
  69.5 15.3 %copy-start.5 = (bf16[768,384]{1,0:T(8,128)(2,1)S(1)}, bf16[768,384]{1,0:T(8,128)(2,1)}, u32[]{:S(2)}) copy-start(bf16[768,384]{1,0:T(8,128)(2,1)} %w_out.1) | copy-start | bytes 1769476
  69.5 15.3 %copy-start.10 = (f32[384]{0:T(512)S(1)}, f32[384]{0:T(512)}, u32[]{:S(2)}) copy-start(f32[384]{0:T(512)} %gain.1) | copy-start | bytes 4612

commit v8 on v7

--- a/solution.py
+++ b/solution.py
@@ -430,19 +430,16 @@
     spread = jnp.mean((value - center) ** 2, axis=-1, keepdims=True)
     normed = (value - center) * lax.rsqrt(spread + 1e-05) * gain[...][None, :]
     hidden = gelu(dot(normed.astype(jnp.bfloat16), w_in[...])).astype(jnp.bfloat16)
-    size = part * lat_rows
     copies = []
-    for top in range(2):
-        cells = slice(top * size, (top + 1) * size)
-        update = value[cells] + dot(hidden[cells], w_out[...])
-        for tile in range(tiles):
-            state[tile, cells, :] = update[:, tile * LANES : (tile + 1) * LANES]
-            for lon in range(part):
-                result[top * part + lon, :, pl.ds(tile * LANES, LANES)] = state[
-                    tile, pl.ds(top * size + lon, lat_rows, stride=part), :
-                ]
-        lons = pl.ds(top * part, part)
-        copies.append(pltpu.make_async_copy(result.at[lons], mixed.at[0, lons], sems.at[top]))
+    for tile in range(tiles):
+        lanes = pl.ds(tile * LANES, LANES)
+        state[tile] = value[:, tile * LANES : (tile + 1) * LANES] + dot(hidden, w_out[:, lanes])
+        for lon in range(lon_cols):
+            first = lon // part * part * lat_rows + lon % part
+            result[lon, :, lanes] = state[tile, pl.ds(first, lat_rows, stride=part), :]
+        copies.append(
+            pltpu.make_async_copy(result.at[:, :, lanes], mixed.at[0, :, :, lanes], sems.at[tile])
+        )
         copies[-1].start()
     for copy in copies:
         copy.wait()
@@ -591,7 +588,7 @@
         scratch_shapes=[
             pltpu.VMEM((channels // LANES, lat_out * lon_out, LANES), jnp.float32),
             pltpu.VMEM((lon_out, lat_out, channels), jnp.float32),
-            pltpu.SemaphoreType.DMA((2,)),
+            pltpu.SemaphoreType.DMA((channels // LANES,)),
         ],
         compiler_params=pltpu.CompilerParams(vmem_limit_bytes=8 * MIB),
         name="mlp",

time: 86.7 us -> 86.8 us (level)
  no operation moved by 1% of the time
where the time goes in v8:
time: 86.8 us; the launch traced here: 86.6 us
  blocking collectives  78 us (90%)
  Pallas kernels  8.29 us (10%)
    all_to_all x4, blocking collectives, exchange(): moved = lax.all_to_all(split, BOTH, split_axis=0, concat_axis=0, tiled=True)  78 us
    pallas_call x1, Pallas kernels, jointly(): pl.pallas_call(scatter_kernel, in_specs=[hbm] * 3, out_specs=[vmem] * 2,...  2.02 us
    pallas_call x1, Pallas kernels, jointly(): pl.pallas_call(functools.partial(synthesis_kernel, polar_count), in_specs...  1.76 us

profile of v8, /device:TPU:0, one launch (start us, length us, event | category | flops | bytes accessed | tf_op | source)
XLA Modules:
  0.0 86.6 jit_solution(12591470780620174340)
XLA Ops:
  0.0 2.0 %scatter_channels.1 = (f32[32,24,384]{2,1,0:T(8,128)S(1)}, f32[2,2,384,384]{3,2,1,0:T(8,128)S(1)}) custom-call(f32[1,32,24,384]{3,2,1,0:T(8,128)} %field.1, f32[8,384,384]{2,1,0:T(8,128)} %real.1, f32[8,384,384]{2,1,0:T(8,128)} %imag.1), custom_call_target="tpu_custom_call" | custom-call | tf_op jit(solution)/shard_map/scatter_channels/pallas_call | solution.py:532
  2.0 0.0 copy-start.2
  2.0 0.0 copy-start.3
  2.1 0.0 copy-start.6
  2.1 0.0 copy-start.7
  2.1 37.5 %all_to_all.20.got = f32[32,24,384]{2,1,0:T(8,128)S(1)} all-to-all(f32[32,24,384]{2,1,0:T(8,128)S(1)} %get-tuple-element.9), channel_id=1, replica_groups=mesh['polar'=4,'azimuth'=8] {'polar','azimuth'}, dimensions={0} | all-to-all | bytes 2359296 | tf_op jit(solution)/shard_map/all_to_all | solution.py:522
  39.6 0.0 copy-done.2
  39.6 0.0 copy-done.3
  39.6 0.0 copy-done.6
  39.6 0.0 copy-done.7
  39.6 0.0 copy-start.1
  39.6 1.5 %analysis.1 = (f32[32,24,128]{2,1,0:T(8,128)S(1)}, f32[576,128]{1,0:T(8,128)S(1)}) custom-call(f32[32,24,384]{2,1,0:T(8,128)S(1)} %all_to_all.20.got, bf16[96,192]{1,0:T(8,128)(2,1)S(1)} %copy-done.7, bf16[96,192]{1,0:T(8,128)(2,1)S(1)} %copy-done.6, bf16[16,128,256]{2,1,0:T(8,128)(2,1)S(1)} %copy-done.3, bf16[16,128,256]{2,1,0:T(8,128)(2,1)S(1)} %copy-done.2), custom_call_target="tpu_custom_call" | custom-call | tf_op jit(solution)/shard_map/analysis/pallas_call | solution.py:549
  41.1 0.0 copy-start
  41.1 0.0 copy-start.8
  41.2 0.0 copy-start.9
  41.2 13.5 %all_to_all.21 = f32[32,9,2,128]{3,2,1,0:T(2,128)S(1)} all-to-all(f32[32,9,2,128]{3,2,1,0:T(2,128)S(1)} %bitcast.12), channel_id=1, replica_groups=mesh['polar'=4,'azimuth'=8] {'polar','azimuth'}, dimensions={0} | all-to-all | bytes 589824 | tf_op jit(solution)/shard_map/all_to_all | solution.py:522
  54.7 1.3 %channel_filter.1 = f32[576,128]{1,0:T(8,128)S(1)} custom-call(f32[576,128]{1,0:T(8,128)S(1)} %bitcast.9, f32[2,2,384,384]{3,2,1,0:T(8,128)S(1)} %get-tuple-element.11.own_filter), custom_call_target="tpu_custom_call" | custom-call | tf_op jit(solution)/shard_map/channel_filter/pallas_call | solution.py:559
  56.0 13.5 %all_to_all.22 = f32[32,9,2,128]{3,2,1,0:T(2,128)S(1)} all-to-all(f32[32,9,2,128]{3,2,1,0:T(2,128)S(1)} %bitcast.10), channel_id=1, replica_groups=mesh['polar'=4,'azimuth'=8] {'polar','azimuth'}, dimensions={0} | all-to-all | bytes 589824 | tf_op jit(solution)/shard_map/all_to_all | solution.py:522
  69.5 0.0 copy-done.1
  69.5 0.0 copy-done
  69.5 0.0 copy-done.8
  69.5 0.0 copy-done.9
  69.5 0.0 copy-start.4
  69.5 0.0 copy-start.5
  69.5 0.0 copy-start.10
  69.5 1.8 %synthesis.1 = f32[576,128]{1,0:T(8,128)S(1)} custom-call(f32[576,128]{1,0:T(8,128)S(1)} %bitcast.7, f32[32,24,128]{2,1,0:T(8,128)S(1)} %get-tuple-element.12.coef, bf16[96,96]{1,0:T(8,128)(2,1)S(1)} %copy-done.9, bf16[96,96]{1,0:T(8,128)(2,1)S(1)} %copy-done.8, bf16[32,128,256]{2,1,0:T(8,128)(2,1)S(1)} %copy-done.1, bf16[32,128,256]{2,1,0:T(8,128)(2,1)S(1)} %copy-done), custom_call_target="tpu_custom_call" | custom-call | tf_op jit(solution)/shard_map/synthesis/pallas_call | solution.py:569
  71.3 13.5 %all_to_all.23 = f32[32,9,2,128]{3,2,1,0:T(2,128)S(1)} all-to-all(f32[32,9,2,128]{3,2,1,0:T(2,128)S(1)} %bitcast.8), channel_id=1, replica_groups=mesh['polar'=4,'azimuth'=8] {'polar','azimuth'}, dimensions={0} | all-to-all | bytes 589824 | tf_op jit(solution)/shard_map/all_to_all | solution.py:522
  84.8 0.0 copy-done.4
  84.8 0.0 copy-done.5
  84.8 0.0 copy-done.10
  84.8 1.7 %mlp.1 = f32[1,12,16,384]{3,2,1,0:T(8,128)} custom-call(f32[576,128]{1,0:T(8,128)S(1)} %bitcast.11, f32[384]{0:T(512)S(1)} %copy-done.10, bf16[384,768]{1,0:T(8,128)(2,1)S(1)} %copy-done.4, bf16[768,384]{1,0:T(8,128)(2,1)S(1)} %copy-done.5), custom_call_target="tpu_custom_call" | custom-call | tf_op jit(solution)/shard_map/mlp/pallas_call | solution.py:583
Async XLA Ops:
  2.0 37.6 %copy-start.2 = (bf16[16,128,256]{2,1,0:T(8,128)(2,1)S(1)}, bf16[16,128,256]{2,1,0:T(8,128)(2,1)}, u32[]{:S(2)}) copy-start(bf16[16,128,256]{2,1,0:T(8,128)(2,1)} %constant.19.clone.leg_low) | copy-start | bytes 3145732
  2.0 37.5 %copy-start.3 = (bf16[16,128,256]{2,1,0:T(8,128)(2,1)S(1)}, bf16[16,128,256]{2,1,0:T(8,128)(2,1)}, u32[]{:S(2)}) copy-start(bf16[16,128,256]{2,1,0:T(8,128)(2,1)} %constant.18.clone.leg_high) | copy-start | bytes 3145732
  2.1 37.5 %copy-start.6 = (bf16[96,192]{1,0:T(8,128)(2,1)S(1)}, bf16[96,192]{1,0:T(8,128)(2,1)}, u32[]{:S(2)}) copy-start(bf16[96,192]{1,0:T(8,128)(2,1)} %constant.17.clone.four_low) | copy-start | bytes 110596
  2.1 37.5 %copy-start.7 = (bf16[96,192]{1,0:T(8,128)(2,1)S(1)}, bf16[96,192]{1,0:T(8,128)(2,1)}, u32[]{:S(2)}) copy-start(bf16[96,192]{1,0:T(8,128)(2,1)} %constant.16.clone.four_high) | copy-start | bytes 110596
  39.6 29.9 %copy-start.1 = (bf16[32,128,256]{2,1,0:T(8,128)(2,1)S(1)}, bf16[32,128,256]{2,1,0:T(8,128)(2,1)}, u32[]{:S(2)}) copy-start(bf16[32,128,256]{2,1,0:T(8,128)(2,1)} %constant.22.clone.leg_high) | copy-start | bytes 6291460
  41.1 28.3 %copy-start = (bf16[32,128,256]{2,1,0:T(8,128)(2,1)S(1)}, bf16[32,128,256]{2,1,0:T(8,128)(2,1)}, u32[]{:S(2)}) copy-start(bf16[32,128,256]{2,1,0:T(8,128)(2,1)} %constant.23.clone.leg_low) | copy-start | bytes 6291460
  41.1 28.3 %copy-start.8 = (bf16[96,96]{1,0:T(8,128)(2,1)S(1)}, bf16[96,96]{1,0:T(8,128)(2,1)}, u32[]{:S(2)}) copy-start(bf16[96,96]{1,0:T(8,128)(2,1)} %constant.21.clone.four_low) | copy-start | bytes 55300
  41.2 28.3 %copy-start.9 = (bf16[96,96]{1,0:T(8,128)(2,1)S(1)}, bf16[96,96]{1,0:T(8,128)(2,1)}, u32[]{:S(2)}) copy-start(bf16[96,96]{1,0:T(8,128)(2,1)} %constant.20.clone.four_high) | copy-start | bytes 55300
  69.5 15.3 %copy-start.4 = (bf16[384,768]{1,0:T(8,128)(2,1)S(1)}, bf16[384,768]{1,0:T(8,128)(2,1)}, u32[]{:S(2)}) copy-start(bf16[384,768]{1,0:T(8,128)(2,1)} %w_in.1) | copy-start | bytes 1769476
  69.5 15.3 %copy-start.5 = (bf16[768,384]{1,0:T(8,128)(2,1)S(1)}, bf16[768,384]{1,0:T(8,128)(2,1)}, u32[]{:S(2)}) copy-start(bf16[768,384]{1,0:T(8,128)(2,1)} %w_out.1) | copy-start | bytes 1769476
  69.5 15.3 %copy-start.10 = (f32[384]{0:T(512)S(1)}, f32[384]{0:T(512)}, u32[]{:S(2)}) copy-start(f32[384]{0:T(512)} %gain.1) | copy-start | bytes 4612
